TPU v7x, 256 devices: a whole 4x4x8 slice. The times are simulated.
256 devices in a mesh: pair: 32 (over x, y, core), edge: 8 (over z).
Axes of the slice: x: 4, y: 4, z: 8, core: 2. Of those that a mesh axis runs over, the one named last changes fastest.
Arguments:
- entities: bfloat16 [64, 2048, 200], P(None, ('pair', 'edge')), may hold values from -5.1 to 5.1
- relations: float32 [4131, 200], replicated, may hold values from -1.5 to 1.5
- edge_src: int32 [32, 32768], P('pair', 'edge'), may hold values from 0 to 2047
- edge_rel: int32 [32, 32768], P('pair', 'edge'), may hold values from 0 to 4130
- edge_dst: int32 [32, 32768], P('pair', 'edge'), may hold values from 0 to 2047
- negatives: int32 [32, 64, 1024], P('pair', 'edge'), may hold values from 0 to 2047
- pair_live: int32 [32], P('pair'), may hold values from 1 to 32768, 524288 in all
- pair_plan: int32 [32, 2], replicated, may hold values from 0 to 63, as said below
Outputs:
- ent_grad: float32 [64, 2048, 200], P(None, ('pair', 'edge'))
- rel_grad: float32 [4131, 200], replicated
Inputs may be any that keep to these rules, and one draw needn't show every extreme that they name: `pair_plan`: each of the 64 partitions appears exactly once in the plan. `pair_live`: one pair has all 32768 slots live.
All inputs are finite; a program needn't handle non-finite values. No bound on the sum of `pair_live` on one device may be relied on, other than what follows from the above.
Results may differ from a plain program's by a relative error of at most 0.00065.
The roundings to bfloat16 on the way count: a program that leaves them out, or rounds other values in their place, can miss the bound.
Values may be sent and summed in bfloat16 or wider, within the bound.
A program may use at most 128 MiB of HBM per device.

v0:
```python
import jax
import jax.numpy as jnp
from jax import lax
from jax.sharding import PartitionSpec as P

DIM = 200
NREL = 4131
PIECE = 8
SPAN = 512
SPANS_DEV = 8


def span_grads(
    source_block, target_block, relations, src_ids, rel_ids, dst_ids, neg_ids, start, live_count
):
    half = relations.shape[1] // 2
    source = source_block[src_ids].astype(jnp.float32)
    target = target_block[dst_ids]
    relation = relations[rel_ids]
    src_re, src_im = (source[:, :half], source[:, half:])
    rel_re, rel_im = (relation[:, :half], relation[:, half:])
    query = jnp.concatenate(
        [src_re * rel_re - src_im * rel_im, src_re * rel_im + src_im * rel_re], axis=1
    ).astype(jnp.bfloat16)
    negative = target_block[neg_ids]
    positive = jnp.sum(query.astype(jnp.float32) * target.astype(jnp.float32), axis=1)
    scores = jnp.dot(query, negative.T, preferred_element_type=jnp.float32)
    peak = jnp.maximum(positive, jnp.max(scores, axis=1))
    pos_exp = jnp.exp(positive - peak)
    neg_exp = jnp.exp(scores - peak[:, None])
    denominator = pos_exp + jnp.sum(neg_exp, axis=1)
    live_mask = (start + jnp.arange(src_ids.shape[0], dtype=jnp.int32) < live_count).astype(
        jnp.float32
    )
    pos_coef = (pos_exp / denominator - 1.0) * live_mask
    weights_b = (neg_exp / denominator[:, None] * live_mask[:, None]).astype(jnp.bfloat16)
    grad_query = pos_coef[:, None] * target.astype(jnp.float32) + jnp.dot(
        weights_b, negative, preferred_element_type=jnp.float32
    )
    grad_neg = jnp.dot(weights_b.T, query, preferred_element_type=jnp.float32)
    grad_pos = pos_coef[:, None] * query.astype(jnp.float32)
    grad_re, grad_im = (grad_query[:, :half], grad_query[:, half:])
    grad_source = jnp.concatenate(
        [grad_re * rel_re + grad_im * rel_im, grad_im * rel_re - grad_re * rel_im], axis=1
    )
    grad_relation = jnp.concatenate(
        [grad_re * src_re + grad_im * src_im, grad_im * src_re - grad_re * src_im], axis=1
    )
    return (grad_source, grad_pos, grad_neg, grad_relation)


def local(entities, relations, edge_src, edge_rel, edge_dst, negatives, pair_live, pair_plan):
    pair_count = lax.axis_size("pair")
    edge_count = lax.axis_size("edge")
    block_rows = PIECE * pair_count * edge_count
    outgoing = entities[jnp.transpose(pair_plan)]
    arrived = lax.all_to_all(outgoing, "pair", split_axis=1, concat_axis=1, tiled=True)
    blocks = lax.all_gather(arrived[:, :, None], "edge", axis=2, tiled=True).reshape(
        2, block_rows, DIM
    )
    source_block = blocks[0]
    target_block = blocks[1]
    records = jnp.stack(
        [
            edge_src[0].reshape(SPANS_DEV, SPAN),
            edge_rel[0].reshape(SPANS_DEV, SPAN),
            edge_dst[0].reshape(SPANS_DEV, SPAN),
        ],
        axis=1,
    )
    samples = negatives[0]
    edge_index = lax.axis_index("edge")
    offsets = jnp.arange(SPANS_DEV, dtype=jnp.int32)
    starts = edge_index * (SPAN * SPANS_DEV) + offsets * SPAN
    live_count = pair_live[0]
    live_blocks = jnp.sum((starts < live_count).astype(jnp.int32))

    def block_step(position, carry):
        src_grad, dst_grad, rel_grad = carry
        record = records[position]
        neg_ids = samples[position]
        grad_source, grad_pos, grad_neg, grad_relation = span_grads(
            source_block,
            target_block,
            relations,
            record[0],
            record[1],
            record[2],
            neg_ids,
            starts[position],
            live_count,
        )
        src_grad = src_grad.at[record[0]].add(grad_source)
        dst_grad = dst_grad.at[record[2]].add(grad_pos).at[neg_ids].add(grad_neg)
        rel_grad = rel_grad.at[record[1]].add(grad_relation)
        return (src_grad, dst_grad, rel_grad)

    empty = jnp.zeros((block_rows, DIM), jnp.float32)
    src_grad, dst_grad, rel_grad = lax.fori_loop(
        0, live_blocks, block_step, (empty, empty, jnp.zeros((NREL, DIM), jnp.float32))
    )
    block_grads = jnp.stack([src_grad, dst_grad])
    shaped = block_grads.reshape(2, pair_count, edge_count * PIECE, DIM)
    moved = lax.all_to_all(shaped, "pair", split_axis=1, concat_axis=1, tiled=True).reshape(
        2, pair_count, edge_count, PIECE, DIM
    )
    returned = lax.psum_scatter(moved, "edge", scatter_dimension=2, tiled=True).reshape(
        2, pair_count, PIECE, DIM
    )
    selector = (
        jnp.transpose(pair_plan)[None] == jnp.arange(2 * pair_count, dtype=jnp.int32)[:, None, None]
    ).astype(jnp.float32)
    ent_grad = jnp.einsum("qsk,skpd->qpd", selector, returned, precision=lax.Precision.HIGHEST)
    rel_final = lax.psum(rel_grad, ("pair", "edge"))
    return (ent_grad, rel_final)


def solution(mesh):
    placed = (
        P(None, ("pair", "edge"), None),
        P(),
        P("pair", "edge"),
        P("pair", "edge"),
        P("pair", "edge"),
        P("pair", "edge", None),
        P("pair"),
        P(),
    )
    return jax.shard_map(
        local,
        mesh=mesh,
        in_specs=placed,
        out_specs=(P(None, ("pair", "edge"), None), P()),
        check_vma=False,
    )
```

profile of v0, /device:TPU:1, one launch (start us, length us, event | category | flops | bytes accessed | tf_op | source)
XLA Modules:
  0.0 1060.8 jit_solution(4672547066761690505)
XLA Ops:
  8.7 17.5 %all_to_all.10 = bf16[2,32,8,200]{3,2,0,1:T(8,128)(2,1)} all-to-all(bf16[2,32,8,200]{3,2,0,1:T(8,128)(2,1)S(1)} %copy.50), channel_id=1, replica_groups=mesh['pair'=32,'edge'=8] {'pair'}, dimensions={1} | all-to-all | bytes 409600 | tf_op jit(solution)/shard_map/all_to_all | solution.py:57
  27.0 5.3 copy.51
  33.1 35.8 %all-gather.3.cloned.1.call-done = bf16[2,32,64,200]{3,2,0,1:T(8,128)(2,1)} async-done(((bf16[2,32,8,200]{3,2,0,1:T(8,128)(2,1)}), bf16[2,32,64,200]{3,2,0,1:T(8,128)(2,1)}) %all-gather.3.cloned.1.call-update) | async-done | bytes 1638416 | tf_op jit(solution)/shard_map/all_gather | solution.py:58
  75.5 587.4 %while.16 = (s32[]{:T(128)}, f32[2048,200]{1,0:T(8,128)}, f32[2048,200]{1,0:T(8,128)S(1)}, f32[4131,200]{1,0:T(8,128)}, s32[]{:T(128)}, /*index=5*/s32[8,3,512]{...) while((s32[]{:T(128)}, f32[2048,200]{1,0:T(8,128)}, ...), condition=%wide.region_9.0_spmd, body=%wide.region_1.0_spmd.sunk | while | flops 637029888 | bytes 38607336 | solution.py:99
  127.4 7.3 scatter_fusion.2
  134.7 6.4 scatter_fusion
  141.1 7.7 scatter_fusion.3
  200.7 7.3 scatter_fusion.2
  208.0 6.4 scatter_fusion
  214.4 7.7 scatter_fusion.3
  274.0 7.3 scatter_fusion.2
  281.3 6.4 scatter_fusion
  287.7 7.7 scatter_fusion.3
  347.3 7.3 scatter_fusion.2
  354.7 6.4 scatter_fusion
  361.0 7.7 scatter_fusion.3
  420.6 7.3 scatter_fusion.2
  428.0 6.4 scatter_fusion
  434.4 7.7 scatter_fusion.3
  494.0 7.3 scatter_fusion.2
  501.3 6.4 scatter_fusion
  507.7 7.7 scatter_fusion.3
  567.3 7.3 scatter_fusion.2
  574.6 6.4 scatter_fusion
  581.0 7.7 scatter_fusion.3
  640.6 7.3 scatter_fusion.2
  647.9 6.4 scatter_fusion
  654.3 7.7 scatter_fusion.3
  664.9 61.6 %all_to_all.11 = f32[2,32,64,200]{3,2,0,1:T(8,128)S(1)} all-to-all(f32[2,32,64,200]{3,2,0,1:T(8,128)S(1)} %pad_maximum_fusion.5), channel_id=1, replica_groups=mesh['pair'=32,'edge'=8] {'pair'}, dimensions={1} | all-to-all | bytes 6553600 | tf_op jit(solution)/shard_map/all_to_all | solution.py:104
  730.9 5.4 copy.53
  736.3 45.2 %reduce-scatter.2.cloned.1.call-done = f32[2,32,1,8,200]{4,1,0,3,2:T(8,128)} async-done(((f32[2,32,8,8,200]{4,1,0,3,2:T(8,128)}), f32[2,32,1,8,200]{4,1,0,3,2:T(8,128)}) %reduce-scatter.2.cloned.1.call-update) | async-done | bytes 409616 | tf_op jit(solution)/shard_map/reduce_scatter | solution.py:107
  784.1 266.2 %all-reduce.2.cloned.1.call-done = f32[4131,200]{0,1:T(8,128)} async-done(((f32[4131,200]{0,1:T(8,128)}), f32[4131,200]{0,1:T(8,128)}) %all-reduce.2.cloned.1.call-update) | async-done | bytes 3304816 | tf_op jit(solution)/shard_map/psum | solution.py:114
  (432 shorter events, 429.9 us)
Async XLA Ops:
  7.2 61.7 %all-gather.3.cloned.1.call-start = ((), (), s32[]{:S(2)}) async-start(), calls=%async_computation.5 | async-start | bytes 2359296 | tf_op jit(solution)/shard_map/all_gather | solution.py:58
  26.3 755.3 %reduce-scatter.2.cloned.1.call-start = ((), (), s32[]{:S(2)}) async-start(), calls=%async_computation.3 | async-start | bytes 4718592 | tf_op jit(solution)/shard_map/reduce_scatter | solution.py:107
  27.0 6.1 copy-start.9
  27.0 6.0 copy-start.10
  27.0 6.0 copy-start.11
  76.2 2.7 copy-start.7
  106.7 7.0 copy-start.3
  109.9 2.0 copy-start.6
  141.1 7.7 copy-start.8
  149.5 2.7 copy-start.7
  180.0 7.0 copy-start.3
  214.4 7.7 copy-start.8
  222.8 2.7 copy-start.7
  253.3 7.0 copy-start.3
  287.7 7.7 copy-start.8
  296.1 2.7 copy-start.7
  326.6 7.0 copy-start.3
  361.0 7.7 copy-start.8
  369.5 2.7 copy-start.7
  399.9 7.0 copy-start.3
  434.4 7.7 copy-start.8
  442.8 2.7 copy-start.7
  473.3 7.0 copy-start.3
  507.7 7.7 copy-start.8
  516.1 2.7 copy-start.7
  546.6 7.0 copy-start.3
  581.0 7.7 copy-start.8
  589.4 2.7 copy-start.7
  619.9 7.0 copy-start.3
  654.3 7.7 copy-start.8
  730.9 319.4 %all-reduce.2.cloned.1.call-start = ((), (), s32[]{:S(2)}) async-start(), calls=%async_computation.4 | async-start | bytes 6758400 | tf_op jit(solution)/shard_map/psum | solution.py:114
  736.3 45.2 %copy-start.12 = (s32[32,2]{0,1:T(2,128)S(1)}, s32[32,2]{0,1:T(2,128)}, u32[]{:S(2)}) copy-start(s32[32,2]{0,1:T(2,128)} %param.17) | copy-start | bytes 772
  (40 other events, 59.0 us)
Sparse Core Ops, SparseCore 0:
  26.4 42.4 all-gather.2
  731.0 50.4 reduce-scatter.1
  787.6 262.7 all-reduce.1
where the time goes:
time: 1070 us; the launch traced here: 1060 us
  waiting for transfers between devices  347 us (32%)
  other arithmetic  304 us (28%)
  local copies, waits for them, and re-layouts  278 us (26%)
  blocking collectives  79.1 us (7%)
  matrix products  30.1 us (3%)
  between operations  14.5 us (1%)
    psum x1, waiting for transfers between devices, local(): rel_final = lax.psum(rel_grad, ('pair', 'edge'))  266 us
    scatter-add x16, other arithmetic, block_step(): dst_grad = dst_grad.at[record[2]].add(grad_pos).at[neg_ids].add(grad_neg)  95 us
    scatter-add x8, other arithmetic, block_step(): rel_grad = rel_grad.at[record[1]].add(grad_relation)  61.6 us
    all_to_all x1, blocking collectives, local(): lax.all_to_all(shaped, 'pair', split_axis=1, concat_axis=1, tiled=True)  61.6 us
    scatter-add x8, other arithmetic, block_step(): src_grad = src_grad.at[record[0]].add(grad_source)  51.1 us
    reduce_scatter x1, waiting for transfers between devices, local(): lax.psum_scatter(moved, 'edge', scatter_dimension=2, tiled=True)  45.2 us
    gather x16, local copies, waits for them, and re-layouts, span_grads(): source = source_block[src_ids].astype(jnp.float32)  42.5 us
    gather x8, local copies, waits for them, and re-layouts, span_grads(): negative = target_block[neg_ids]  39.8 us
  transfers between devices with their start and end apart: 3, of which 3 were waited for; matrix products, arithmetic and copies ran while one was open for 1% of the time, Pallas kernels for 0%

commit v1 on v0

v1 whole, which is shorter than its diff:
```python
import functools
import jax
import jax.numpy as jnp
from jax import lax
from jax.experimental import pallas as pl
from jax.experimental.pallas import tpu as pltpu
from jax.sharding import PartitionSpec as P

DIM = 200
HALF = 100
HPAD = 104
FEAT = 208
NREL = 4131
RTILE = 256
RTILES = 17
SPAN = 512
SPANS_DEV = 8
SLOTS = SPAN * SPANS_DEV
ROWS = 2048
CHUNK = 256
NN = (((1,), (0,)), ((), ()))
NT = (((1,), (1,)), ((), ()))


def mm(a, b, dims=NN):
    return lax.dot_general(a, b, dims, preferred_element_type=jnp.float32)


def split2(v):
    hi = v.astype(jnp.bfloat16)
    lo = (v - hi.astype(jnp.float32)).astype(jnp.bfloat16)
    return jnp.concatenate([hi, lo], axis=0)


def edge_kernel(
    meta_ref, relid_ref, pos_ref, tile_ref,
    src_ref, dst_ref, neg_ref, relf_ref, s_ref, t_ref, table_ref,
    ent_ref, rel_ref,
    tn_ref, sc_ref, w_ref, ohs_ref, ohd_ref, ct_ref, rows_ref, perm_ref, sort_ref,
):
    live_blocks = meta_ref[0]
    live_here = meta_ref[1]
    ent_ref[...] = jnp.zeros_like(ent_ref)
    for h in range(ROWS // CHUNK):
        part = t_ref[:, h * CHUNK:(h + 1) * CHUNK].astype(jnp.float32)
        part = jnp.concatenate([part, jnp.zeros((256 - FEAT, CHUNK), jnp.float32)], axis=0)
        tn_ref[h * CHUNK:(h + 1) * CHUNK, :] = part.T.astype(jnp.bfloat16)

    def block(b, carry):
        def fetch_row(j, c):
            rows_ref[j] = table_ref[relid_ref[b * SPAN + j]]
            return c

        lax.fori_loop(0, SPAN, fetch_row, 0, unroll=16)
        src_row = src_ref[b]
        dst_row = dst_ref[b]
        neg_row = neg_ref[b]
        for h in range(ROWS // CHUNK):
            ids = lax.broadcasted_iota(jnp.int32, (CHUNK, SPAN), 0) + h * CHUNK
            at = pl.ds(h * CHUNK, CHUNK)
            ohs_ref[at, :] = jnp.where(ids == src_row, 1.0, 0.0).astype(jnp.bfloat16)
            ohd_ref[at, :] = jnp.where(ids == dst_row, 1.0, 0.0).astype(jnp.bfloat16)
        neg_hi = neg_row // 128
        neg_lo = neg_row - neg_hi * 128
        oh_hi = jnp.where(lax.broadcasted_iota(jnp.int32, (16, 1024), 0) == neg_hi, 1.0, 0.0).astype(jnp.bfloat16)
        oh_lo = jnp.where(lax.broadcasted_iota(jnp.int32, (128, 1024), 0) == neg_lo, 1.0, 0.0).astype(jnp.bfloat16)
        counts = mm(oh_hi, oh_lo, NT)
        counts_t = mm(oh_lo, oh_hi, NT)
        for h in range(16):
            at = slice(h * 128, (h + 1) * 128)
            scaled = t_ref[:, at].astype(jnp.float32) * counts[h:h + 1, :]
            ct_ref[:, at] = split2(scaled)

        source = mm(s_ref[...], ohs_ref[...])
        target = mm(t_ref[...], ohd_ref[...])
        x = rows_ref[:, 0, :].T[:HPAD]
        y = rows_ref[:, 1, :].T[:HPAD]
        a, c = source[:HPAD], source[HPAD:]
        query_b = jnp.concatenate(
            [a * x - c * y, a * y + c * x, jnp.zeros((256 - FEAT, SPAN), jnp.float32)], axis=0
        ).astype(jnp.bfloat16)
        query = query_b[:FEAT].astype(jnp.float32)
        positive = jnp.sum(query * target, axis=0, keepdims=True)
        peak = positive
        for h in range(8):
            at = slice(h * CHUNK, (h + 1) * CHUNK)
            count = jnp.concatenate([counts_t[:, 2 * h:2 * h + 1], counts_t[:, 2 * h + 1:2 * h + 2]], axis=0)
            scores = mm(tn_ref[at, :], query_b)
            scores = jnp.where(count > 0.0, scores, -1e30)
            sc_ref[at, :] = scores
            peak = jnp.maximum(peak, jnp.max(scores, axis=0, keepdims=True))
        pos_exp = jnp.exp(positive - peak)
        total = pos_exp
        for h in range(8):
            at = slice(h * CHUNK, (h + 1) * CHUNK)
            count = jnp.concatenate([counts_t[:, 2 * h:2 * h + 1], counts_t[:, 2 * h + 1:2 * h + 2]], axis=0)
            e = jnp.exp(sc_ref[at, :] - peak)
            sc_ref[at, :] = e
            total = total + jnp.sum(e * count, axis=0, keepdims=True)
        inv = 1.0 / total
        live = jnp.where(
            lax.broadcasted_iota(jnp.int32, (1, SPAN), 1) + b * SPAN < live_here, 1.0, 0.0
        )
        coef = (pos_exp * inv - 1.0) * live
        inv = inv * live
        for h in range(8):
            at = slice(h * CHUNK, (h + 1) * CHUNK)
            w_ref[at, :] = (sc_ref[at, :] * inv).astype(jnp.bfloat16)
        both = mm(ct_ref[...], w_ref[...])
        grad_q = both[:FEAT] + both[FEAT:] + coef * target
        pos_q = split2(coef * query)
        g, k = grad_q[:HPAD], grad_q[HPAD:]
        grad_s = split2(jnp.concatenate([g * x + k * y, k * x - g * y], axis=0))
        relrow = relf_ref[b]
        first = lax.broadcasted_iota(jnp.int32, (24, SPAN), 0) == 0
        perm_ref[:, 0, :] = jnp.concatenate(
            [g * a + k * c, jnp.where(first, relrow, 0.0)], axis=0
        ).T
        perm_ref[:, 1, :] = jnp.concatenate(
            [k * a - g * c, jnp.zeros((24, SPAN), jnp.float32)], axis=0
        ).T

        def place_row(j, cc):
            sort_ref[pos_ref[b * SPAN + j]] = perm_ref[j]
            return cc

        lax.fori_loop(0, SPAN, place_row, 0, unroll=16)
        for h in range(8):
            at = slice(h * CHUNK, (h + 1) * CHUNK)
            oh = ohs_ref[at, :]
            back = mm(grad_s, oh, NT)
            ent_ref[:FEAT, at] += back[:FEAT] + back[FEAT:]
            neg = mm(query_b[:FEAT], w_ref[at, :], NT)
            pos = mm(pos_q, ohd_ref[at, :], NT)
            count = jnp.concatenate([counts[2 * h:2 * h + 1, :], counts[2 * h + 1:2 * h + 2, :]], axis=1)
            ent_ref[FEAT:, at] += neg * count + (pos[:FEAT] + pos[FEAT:])
        return carry

    lax.fori_loop(0, live_blocks, block, 0)

    def tile(t, carry):
        begin = tile_ref[t]
        size = tile_ref[RTILES + t]

        def piece(n, acc):
            base = begin + n * RTILE
            left = size - n * RTILE
            ok = lax.broadcasted_iota(jnp.int32, (RTILE, 128), 0) < left
            re = jnp.where(ok, sort_ref[pl.ds(base, RTILE), 0, :], 0.0).T
            im = jnp.where(ok, sort_ref[pl.ds(base, RTILE), 1, :], 0.0).T
            names = re[HPAD:HPAD + 1, :].astype(jnp.int32)
            oh = jnp.where(
                lax.broadcasted_iota(jnp.int32, (RTILE, RTILE), 0) + t * RTILE == names, 1.0, 0.0
            ).astype(jnp.bfloat16)
            part = mm(split2(jnp.concatenate([re[:HPAD], im[:HPAD]], axis=0)), oh, NT)
            return acc + part[:FEAT] + part[FEAT:]

        acc = lax.fori_loop(
            0, (size + RTILE - 1) // RTILE, piece, jnp.zeros((FEAT, RTILE), jnp.float32)
        )
        rel_ref[:, pl.ds(pl.multiple_of(t * RTILE, RTILE), RTILE)] = acc
        return carry

    lax.fori_loop(0, RTILES, tile, 0)


def edge_call(meta, relid, pos, tiles, src, dst, neg, relf, s_t, t_t, table):
    smem = pl.BlockSpec(memory_space=pltpu.SMEM)
    vmem = pl.BlockSpec(memory_space=pltpu.VMEM)
    return pl.pallas_call(
        edge_kernel,
        out_shape=(
            jax.ShapeDtypeStruct((2 * FEAT, ROWS), jnp.float32),
            jax.ShapeDtypeStruct((FEAT, RTILES * RTILE), jnp.float32),
        ),
        in_specs=[smem] * 4 + [vmem] * 7,
        out_specs=(vmem, vmem),
        scratch_shapes=[
            pltpu.VMEM((ROWS, 256), jnp.bfloat16),
            pltpu.VMEM((ROWS, SPAN), jnp.float32),
            pltpu.VMEM((ROWS, SPAN), jnp.bfloat16),
            pltpu.VMEM((ROWS, SPAN), jnp.bfloat16),
            pltpu.VMEM((ROWS, SPAN), jnp.bfloat16),
            pltpu.VMEM((2 * FEAT, ROWS), jnp.bfloat16),
            pltpu.VMEM((SPAN, 2, 128), jnp.float32),
            pltpu.VMEM((SPAN, 2, 128), jnp.float32),
            pltpu.VMEM((SLOTS + RTILE, 2, 128), jnp.float32),
        ],
        compiler_params=pltpu.CompilerParams(vmem_limit_bytes=56 * 1024 * 1024),
        name="edges",
    )(meta, relid, pos, tiles, src, dst, neg, relf, s_t, t_t, table)


def place(ids):
    return ((ids >> 3) & 7) * 256 + (ids >> 6) * 8 + (ids & 7)


def bucket(relid, live_blocks):
    which = relid >> 8
    valid = (jnp.arange(SLOTS, dtype=jnp.int32) < live_blocks * SPAN)[:, None]
    one = ((which[:, None] == jnp.arange(RTILES, dtype=jnp.int32)[None]) & valid).astype(jnp.bfloat16)
    grid = one.reshape(SLOTS // 128, 128, RTILES)
    tri = (jnp.arange(128)[:, None] > jnp.arange(128)[None]).astype(jnp.bfloat16)
    inner = jnp.einsum("ij,cjt->cit", tri, grid, preferred_element_type=jnp.float32)
    sums = jnp.sum(grid.astype(jnp.float32), axis=1)
    outer = jnp.cumsum(sums, axis=0) - sums
    size = jnp.sum(sums, axis=0)
    begin = jnp.cumsum(size) - size
    where = inner + (outer + begin[None])[:, None, :]
    pos = jnp.sum(where * grid.astype(jnp.float32), axis=2).reshape(SLOTS).astype(jnp.int32)
    return pos, jnp.concatenate([begin, size]).astype(jnp.int32)


def halves(v):
    pad = [(0, 0)] * (v.ndim - 1) + [(0, HPAD - HALF)]
    return jnp.concatenate([jnp.pad(v[..., :HALF], pad), jnp.pad(v[..., HALF:], pad)], axis=-1)


def rel_table(relations):
    return jnp.pad(relations.reshape(NREL, 2, HALF), ((0, 0), (0, 0), (0, 128 - HALF)))


def edge_work(s_t, t_t, relations, edge_src, edge_rel, edge_dst, negatives, live_count, first_slot):
    live_here = live_count - first_slot
    live_blocks = jnp.clip((live_here + SPAN - 1) // SPAN, 0, SPANS_DEV)
    meta = jnp.stack([live_blocks, live_here])
    pos, tiles = bucket(edge_rel, live_blocks)
    return edge_call(
        meta, edge_rel, pos, tiles,
        place(edge_src).reshape(SPANS_DEV, 1, SPAN),
        place(edge_dst).reshape(SPANS_DEV, 1, SPAN),
        place(negatives).reshape(SPANS_DEV, 1, 1024),
        edge_rel.astype(jnp.float32).reshape(SPANS_DEV, 1, SPAN),
        s_t, t_t, rel_table(relations),
    )


def unhalve(v):
    return jnp.concatenate([v[..., :HALF], v[..., HPAD:HPAD + HALF]], axis=-1)


def local(entities, relations, edge_src, edge_rel, edge_dst, negatives, pair_live, pair_plan):
    pair_count = lax.axis_size("pair")
    edge_index = lax.axis_index("edge")
    outgoing = halves(entities[jnp.transpose(pair_plan)])
    arrived = lax.all_to_all(outgoing, "pair", split_axis=1, concat_axis=1, tiled=True)
    owned = jnp.transpose(arrived.reshape(2, CHUNK, FEAT), (0, 2, 1))
    blocks = lax.all_gather(owned, "edge", axis=2, tiled=True)
    ent, rel = edge_work(
        blocks[0], blocks[1], relations, edge_src[0], edge_rel[0], edge_dst[0], negatives[0],
        pair_live[0], edge_index * SLOTS,
    )
    summed = lax.psum_scatter(ent, "edge", scatter_dimension=1, tiled=True)
    rows = jnp.transpose(summed.reshape(2, FEAT, CHUNK), (0, 2, 1)).reshape(2, pair_count, 8, FEAT)
    returned = lax.all_to_all(rows, "pair", split_axis=1, concat_axis=1, tiled=True)
    where = jnp.argsort(jnp.transpose(pair_plan).reshape(-1))
    ent_grad = unhalve(returned.reshape(2 * pair_count, 8, FEAT)[where])
    rel_grad = lax.psum(unhalve(rel.T)[:NREL], ("pair", "edge"))
    return ent_grad, rel_grad


def solution(mesh):
    placed = (
        P(None, ("pair", "edge"), None),
        P(),
        P("pair", "edge"),
        P("pair", "edge"),
        P("pair", "edge"),
        P("pair", "edge", None),
        P("pair"),
        P(),
    )
    return jax.shard_map(
        local,
        mesh=mesh,
        in_specs=placed,
        out_specs=(P(None, ("pair", "edge"), None), P()),
        check_vma=False,
    )
```

time: 1070 us -> 498 us (0.47)
  other arithmetic: 304 us -> 12.4 us
  local copies, waits for them, and re-layouts: 278 us -> 32.8 us
  Pallas kernels: 0 us -> 93.5 us
  blocking collectives: 79.1 us -> 0 us
  matrix products: 30.1 us -> 0.21 us
  waiting for transfers between devices: 347 us -> 327 us
  starting transfers between devices: 0.12 us -> 16.4 us
    scatter-add x32 -> x0, other arithmetic: 208 us -> none  [the longest x16 95 us: block_step(): dst_grad = dst_grad.at[record[2]].add(grad_pos).at[neg_ids].add(grad_neg)]
    gather x50 -> x2, local copies, waits for them, and re-layouts: 153 us -> 1.22 us  [the longest x1 0.63 us: local(): ent_grad = unhalve(returned.reshape(2 * pair_count, 8, FEAT)[where])]
    pallas_call x0 -> x1, Pallas kernels: none -> 93.5 us  [edge_call(): pl.pallas_call(edge_kernel, out_shape=(jax.ShapeDtypeStruct((2 * FEAT, RO...]
    all_to_all x2 -> x0, blocking collectives: 79.1 us -> none  [the longest x1 61.6 us: local(): lax.all_to_all(shaped, 'pair', split_axis=1, concat_axis=1, tiled=True)]
    while x146 -> x0, local copies, waits for them, and re-layouts: 39.3 us -> none
    concatenate x16 -> x1, local copies, waits for them, and re-layouts: 32.1 us -> 0.72 us  [halves(): jnp.concatenate([jnp.pad(v[..., :HALF], pad), jnp.pad(v[..., HALF:], pad)...]
    dot_general x25 -> x1, matrix products: 30.1 us -> 0.21 us  [bucket(): jnp.einsum('ij,cjt->cit', tri, grid, preferred_element_type=jnp.float32)]
    convert_element_type x24 -> x3, other arithmetic: 28.7 us -> 2.7 us  [the longest x1 1.43 us: edge_work(): edge_rel.astype(jnp.float32).reshape(SPANS_DEV, 1, SPAN)]
  transfers between devices with their start and end apart: 3 -> 5, of which waited for: 3 -> 5; matrix products, arithmetic and copies ran while one was open for 1% -> 7% of each run, Pallas kernels for 0% -> 0%
where the time goes in v1:
time: 498 us; the launch traced here: 496 us
  waiting for transfers between devices  327 us (66%)
  Pallas kernels  93.5 us (19%)
  local copies, waits for them, and re-layouts  32.8 us (7%)
  starting transfers between devices  16.4 us (3%)
  between operations  14.6 us (3%)
  other arithmetic  12.4 us (2%)
    psum x1, waiting for transfers between devices, local(): rel_grad = lax.psum(unhalve(rel.T)[:NREL], ('pair', 'edge'))  246 us
    pallas_call x1, Pallas kernels, edge_call(): pl.pallas_call(edge_kernel, out_shape=(jax.ShapeDtypeStruct((2 * FEAT, RO...  93.5 us
    reduce_scatter x1, waiting for transfers between devices, local(): summed = lax.psum_scatter(ent, 'edge', scatter_dimension=1, tiled=True)  47.3 us
    all_gather x1, waiting for transfers between devices, local(): blocks = lax.all_gather(owned, 'edge', axis=2, tiled=True)  16.6 us
    reshape x2, local copies, waits for them, and re-layouts, rel_table(): relations.reshape(NREL, 2, HALF)  11.6 us
  transfers between devices with their start and end apart: 5, of which 5 were waited for; matrix products, arithmetic and copies ran while one was open for 7% of the time, Pallas kernels for 0%

profile of v1, /device:TPU:1, one launch (start us, length us, event | category | flops | bytes accessed | tf_op | source)
XLA Modules:
  0.0 496.4 jit_solution(8551593989517728862)
XLA Ops:
  7.2 0.7 compare_select_fusion
  8.1 0.6 gather_fusion
  8.8 0.7 slice_select_fusion
  9.7 0.7 copy.46
  10.4 8.6 %all-to-all-start = ((bf16[2,32,8,208]{3,2,0,1:T(8,128)(2,1)}), bf16[2,32,8,208]{3,2,0,1:T(8,128)(2,1)S(1)}, u32[]{:S(2)}, u32[]{:S(2)}) async-start(bf16[2,32,8,208]{3,2,0,1:T(8,128)(2,1)} %copy.46), calls=%async_computation | async-start | bytes 524288 | tf_op jit(solution)/shard_map/all_to_all | solution.py:246
  19.0 1.4 fusion.14
  21.1 6.8 %all-to-all-done = bf16[2,32,8,208]{3,2,0,1:T(8,128)(2,1)S(1)} async-done(((bf16[2,32,8,208]{3,2,0,1:T(8,128)(2,1)}), bf16[2,32,8,208]{3,2,0,1:T(8,128)(2,1)S(1)}, u32[]{:S(2)}, u32[]{:S(2)}) %all-to-all-start) | async-done | bytes 213024 | tf_op jit(solution)/shard_map/all_to_all | solution.py:246
  28.0 0.8 copy.48
  29.7 4.1 reshape.292
  33.7 7.5 %copy.49 = f32[4131,2,100]{2,1,0:T(2,128)} copy(f32[4131,2,100]{0,2,1:T(8,128)} %reshape.292) | data formatting | bytes 6609600 | tf_op jit(solution)/shard_map/reshape | solution.py:220
  41.2 6.6 %pad.13.table_ref = f32[4131,2,128]{2,1,0:T(2,128)} pad(f32[4131,2,100]{2,1,0:T(2,128)} %copy.49, f32[]{:T(128)} %constant.55.clone.1), padding=0_0x0_0x0_28 | pad | bytes 7534948 | tf_op jit(solution)/shard_map/jit(_pad)/pad | solution.py:220
  47.8 0.7 maximum_convert_fusion.tile_ref
  48.4 0.6 pad_add_fusion.meta_ref
  49.3 0.6 convert_bitcast_fusion.pos_ref
  49.9 0.7 add_bitcast_fusion.neg_ref
  50.6 0.6 and_add_fusion
  51.2 0.6 and_add_fusion.1
  51.9 16.6 %all-gather.2.cloned.1.call-done = bf16[2,208,2048]{2,1,0:T(8,128)(2,1)} async-done(((bf16[2,208,256]{2,1,0:T(8,128)(2,1)}), bf16[2,208,2048]{2,1,0:T(8,128)(2,1)}) %all-gather.2.cloned.1.call-update) | async-done | bytes 1703952 | tf_op jit(solution)/shard_map/all_gather | solution.py:248
  68.4 2.8 slice_bitcast_fusion
  71.2 93.5 %edges.1 = (f32[416,2048]{1,0:T(8,128)}, f32[208,4352]{1,0:T(8,128)}) custom-call(s32[2]{0:T(128)} %pad_add_fusion.meta_ref, s32[4096]{0:T(1024)} %bitcast.50, s32[4096]{0:T(1024)} %convert_bitcast_fusion.pos_ref, s32[34]{0:T(128)} %maximum_convert_fusion.tile_ref, s32[8,1,512]{2,1,0:T(1,128)} %bitcast.53, s32[8,1,512]{2,1,0:T(1,128)} %bitcast.52, ...), custom_call_target="tpu_custom_call" | custom-call | tf_op jit(solution)/shard_map/edges/pallas_call | solution.py:170
  164.7 2.3 fusion.12
  167.0 2.0 pad_maximum_fusion
  169.0 47.3 %reduce-scatter.2.cloned.1.call-done = f32[416,256]{1,0:T(8,128)} async-done(((f32[416,2048]{1,0:T(8,128)}), f32[416,256]{1,0:T(8,128)}) %reduce-scatter.2.cloned.1.call-update) | async-done | bytes 426000 | tf_op jit(solution)/shard_map/reduce_scatter | solution.py:253
  216.4 1.2 copy.50
  217.6 0.9 copy.51
  218.4 7.7 %all-to-all-start.1 = ((f32[2,32,8,208]{3,2,0,1:T(8,128)}), f32[2,32,8,208]{3,2,0,1:T(8,128)S(1)}, u32[]{:S(2)}, u32[]{:S(2)}) async-start(f32[2,32,8,208]{3,2,0,1:T(8,128)} %copy.51), calls=%async_computation.2 | async-start | bytes 1048576 | tf_op jit(solution)/shard_map/all_to_all | solution.py:255
  226.2 2.1 sort.17
  228.3 9.4 %all-to-all-done.1 = f32[2,32,8,208]{3,2,0,1:T(8,128)S(1)} async-done(((f32[2,32,8,208]{3,2,0,1:T(8,128)}), f32[2,32,8,208]{3,2,0,1:T(8,128)S(1)}, u32[]{:S(2)}, u32[]{:S(2)}) %all-to-all-start.1) | async-done | bytes 426016 | tf_op jit(solution)/shard_map/all_to_all | solution.py:255
  237.8 0.6 gather_fusion.1
  238.6 1.0 pad_maximum_fusion.1
  239.6 246.4 %all-reduce.4.cloned.1.call-done = f32[4131,200]{0,1:T(8,128)} async-done(((f32[4131,200]{0,1:T(8,128)}), f32[4131,200]{0,1:T(8,128)}) %all-reduce.4.cloned.1.call-update) | async-done | bytes 3304816 | tf_op jit(solution)/shard_map/psum | solution.py:258
  486.0 3.9 copy.58
  (38 shorter events, 1.9 us)
Async XLA Ops:
  7.2 1.0 copy-start
  10.4 17.6 %all-to-all-start = ((bf16[2,32,8,208]{3,2,0,1:T(8,128)(2,1)}), bf16[2,32,8,208]{3,2,0,1:T(8,128)(2,1)S(1)}, u32[]{:S(2)}, u32[]{:S(2)}) async-start(bf16[2,32,8,208]{3,2,0,1:T(8,128)(2,1)} %copy.46), calls=%async_computation | async-start | bytes 524288 | tf_op jit(solution)/shard_map/all_to_all | solution.py:246
  19.0 49.4 %all-gather.2.cloned.1.call-start = ((), (), s32[]{:S(2)}) async-start(), calls=%async_computation.3 | async-start | bytes 1916928 | tf_op jit(solution)/shard_map/all_gather | solution.py:248
  28.8 187.5 %reduce-scatter.2.cloned.1.call-start = ((), (), s32[]{:S(2)}) async-start(), calls=%async_computation.4 | async-start | bytes 3833856 | tf_op jit(solution)/shard_map/reduce_scatter | solution.py:253
  41.2 8.7 %copy-start.1 = (s32[1,8,1024]{2,1,0:T(8,128)S(1)}, s32[1,8,1024]{2,1,0:T(8,128)}, u32[]{:S(2)}) copy-start(s32[1,8,1024]{2,1,0:T(8,128)} %param.13) | copy-start | bytes 98308
  41.2 9.4 %copy-start.2 = (s32[1,4096]{1,0:T(1,128)S(1)}, s32[1,4096]{1,0:T(1,128)}, u32[]{:S(2)}) copy-start(s32[1,4096]{1,0:T(1,128)} %param.12) | copy-start | bytes 49156
  41.2 10.0 %copy-start.3 = (s32[1,4096]{1,0:T(1,128)S(1)}, s32[1,4096]{1,0:T(1,128)}, u32[]{:S(2)}) copy-start(s32[1,4096]{1,0:T(1,128)} %param.10) | copy-start | bytes 49156
  164.7 321.3 %all-reduce.4.cloned.1.call-start = ((), (), s32[]{:S(2)}) async-start(), calls=%async_computation.5 | async-start | bytes 6758400 | tf_op jit(solution)/shard_map/psum | solution.py:258
  169.0 57.1 %copy-start.4 = (s32[32,2]{0,1:T(2,128)S(1)}, s32[32,2]{0,1:T(2,128)}, u32[]{:S(2)}) copy-start(s32[32,2]{0,1:T(2,128)} %param.15) | copy-start | bytes 772
  218.4 19.3 %all-to-all-start.1 = ((f32[2,32,8,208]{3,2,0,1:T(8,128)}), f32[2,32,8,208]{3,2,0,1:T(8,128)S(1)}, u32[]{:S(2)}, u32[]{:S(2)}) async-start(f32[2,32,8,208]{3,2,0,1:T(8,128)} %copy.51), calls=%async_computation.2 | async-start | bytes 1048576 | tf_op jit(solution)/shard_map/all_to_all | solution.py:255
Sparse Core Ops, SparseCore 0:
  29.0 39.4 all-gather.1
  164.8 51.4 reduce-scatter.1
  222.4 263.5 all-reduce.3

commit v2 on v1

--- a/solution.py
+++ b/solution.py
@@ -20,6 +20,7 @@
 CHUNK = 256
 NN = (((1,), (0,)), ((), ()))
 NT = (((1,), (1,)), ((), ()))
+MESH = pl.DeviceIdType.MESH
 
 
 def mm(a, b, dims=NN):
@@ -129,11 +130,11 @@
             at = slice(h * CHUNK, (h + 1) * CHUNK)
             oh = ohs_ref[at, :]
             back = mm(grad_s, oh, NT)
-            ent_ref[:FEAT, at] += back[:FEAT] + back[FEAT:]
+            ent_ref[h, :FEAT, :] += back[:FEAT] + back[FEAT:]
             neg = mm(query_b[:FEAT], w_ref[at, :], NT)
             pos = mm(pos_q, ohd_ref[at, :], NT)
             count = jnp.concatenate([counts[2 * h:2 * h + 1, :], counts[2 * h + 1:2 * h + 2, :]], axis=1)
-            ent_ref[FEAT:, at] += neg * count + (pos[:FEAT] + pos[FEAT:])
+            ent_ref[h, FEAT:, :] += neg * count + (pos[:FEAT] + pos[FEAT:])
         return carry
 
     lax.fori_loop(0, live_blocks, block, 0)
@@ -158,10 +159,12 @@
         acc = lax.fori_loop(
             0, (size + RTILE - 1) // RTILE, piece, jnp.zeros((FEAT, RTILE), jnp.float32)
         )
-        rel_ref[:, pl.ds(pl.multiple_of(t * RTILE, RTILE), RTILE)] = acc
+        rel_ref[pl.ds(52 * t, 26)] = acc[:, :128].reshape(26, 8, 128)
+        rel_ref[pl.ds(52 * t + 26, 26)] = acc[:, 128:].reshape(26, 8, 128)
         return carry
 
     lax.fori_loop(0, RTILES, tile, 0)
+    rel_ref[884:] = jnp.zeros((12, 8, 128), jnp.float32)
 
 
 def edge_call(meta, relid, pos, tiles, src, dst, neg, relf, s_t, t_t, table):
@@ -170,8 +173,8 @@
     return pl.pallas_call(
         edge_kernel,
         out_shape=(
-            jax.ShapeDtypeStruct((2 * FEAT, ROWS), jnp.float32),
-            jax.ShapeDtypeStruct((FEAT, RTILES * RTILE), jnp.float32),
+            jax.ShapeDtypeStruct((8, 2 * FEAT, CHUNK), jnp.float32),
+            jax.ShapeDtypeStruct((896, 8, 128), jnp.float32),
         ),
         in_specs=[smem] * 4 + [vmem] * 7,
         out_specs=(vmem, vmem),
@@ -235,12 +238,264 @@
     )
 
 
-def unhalve(v):
-    return jnp.concatenate([v[..., :HALF], v[..., HPAD:HPAD + HALF]], axis=-1)
+RINGS = 104
+TILE7 = 7
+
+
+def exchange_kernel(
+    g_ref, r_ref, ent_ref, rel_ref,
+    ring_ref, core_ref, acc_ref, hyp_ref, zb_ref, zr_ref, zf_ref, out_ref,
+    ring_s, ring_r, core_s, core_r, hyp_s, hyp_r, zs_s, zs_r, za_s, za_r,
+    ag_s, ag_r, last_s, last_r, a2a_s, a2a_r,
+):
+    p = lax.axis_index("pair")
+    e = lax.axis_index("edge")
+    core = p % 2
+    chip = p // 2
+    x = chip // 4
+    y = chip % 4
+
+    def at(xx, yy):
+        return ((xx * 4 + yy) * 2 + core, e)
+
+    partner = {
+        "x1": at(x + 1 - 2 * (x % 2), y),
+        "x2": at(3 - x, y),
+        "y1": at(x, y + 1 - 2 * (y % 2)),
+        "y2": at(x, 3 - y),
+    }
+    bit = {
+        "x1": (x // 2 + x % 2) % 2,
+        "x2": x // 2,
+        "y1": (y // 2 + y % 2) % 2,
+        "y2": y // 2,
+    }
+    order = [
+        ("x1", "y1", "x2", "y2"),
+        ("y1", "x2", "y2", "x1"),
+        ("x2", "y2", "x1", "y1"),
+        ("y2", "x1", "y1", "x2"),
+    ]
+    sibling = (p + 1 - 2 * core, e)
+
+    barrier = pltpu.get_barrier_semaphore()
+    for d in range(1, 32):
+        pl.semaphore_signal(barrier, inc=1, device_id=((p + d) % 32, e), device_id_type=MESH)
+    for d in range(1, 8):
+        pl.semaphore_signal(barrier, inc=1, device_id=(p, (e + d) % 8), device_id_type=MESH)
+    pl.semaphore_wait(barrier, 38)
+
+    sent = []
+
+    def push(src, dst, ss, rs, device):
+        copy = pltpu.make_async_remote_copy(
+            src_ref=src, dst_ref=dst, send_sem=ss, recv_sem=rs, device_id=device, device_id_type=MESH
+        )
+        copy.start()
+        sent.append(copy)
+        return copy
+
+    streams = [(0, 0), (208, 1), (104, 0), (312, 1)]
+    ring = {}
+
+    def chunk(down, s):
+        return (e + 1 + s) % 8 if down else (e + 7 - s) % 8
+
+    def ring_send(s):
+        for i, (row, down) in enumerate(streams):
+            c = chunk(down, s)
+            if s == 0:
+                src = g_ref.at[c, pl.ds(row, RINGS)]
+            else:
+                ring[i].wait_recv()
+                ring_ref[i, s - 1] += g_ref[c, pl.ds(row, RINGS), :]
+                src = ring_ref.at[i, s - 1]
+            to = (p, (e + 7) % 8) if down else (p, (e + 1) % 8)
+            ring[i] = push(src, ring_ref.at[i, s], ring_s.at[i, s], ring_r.at[i, s], to)
+
+    moves = {}
+    off = [0, 0, 0, 0]
+    offs = [[], [], [], []]
+    base = [0, 8, 12, 14]
+
+    def hyp_send(k, s):
+        half = 8 >> s
+        b = bit[order[k][s]]
+        moves[k] = push(
+            acc_ref.at[k, pl.ds(off[k] + (1 - b) * half, half)],
+            hyp_ref.at[k, pl.ds(base[s], half)],
+            hyp_s.at[k, s], hyp_r.at[k, s], partner[order[k][s]],
+        )
+        off[k] = off[k] + b * half
+        offs[k].append(off[k])
+
+    def hyp_take(k, s):
+        half = 8 >> s
+        moves[k].wait_recv()
+        acc_ref[k, pl.ds(off[k], half)] += hyp_ref[k, pl.ds(base[s], half)]
+
+    cores = [
+        push(r_ref.at[1 - core, k], core_ref.at[k], core_s.at[k], core_r.at[k], sibling)
+        for k in range(4)
+    ]
+    ring_send(0)
+    for k in range(4):
+        cores[k].wait_recv()
+        acc_ref[k] = r_ref[core, k] + core_ref[k]
+        hyp_send(k, 0)
+    ring_send(1)
+
+    def hyp_step(s):
+        for k in range(4):
+            hyp_take(k, s)
+            if s < 3:
+                hyp_send(k, s + 1)
+
+    hyp_step(0)
+    ring_send(2)
+    hyp_step(1)
+    hyp_step(2)
+    ring_send(3)
+    hyp_step(3)
+    for t in range(TILE7):
+        for k in range(4):
+            zb_ref[t, k] = acc_ref[k, off[k], t]
+    zb_ref[TILE7] = jnp.zeros((4, 8, 128), jnp.float32)
+    zs = [
+        push(zb_ref.at[(e + d) % 8], zr_ref.at[d], zs_s.at[d], zs_r.at[d], (p, (e + d) % 8))
+        for d in range(1, 8)
+    ]
+    ring_send(4)
+    total = zb_ref[e]
+    for d in range(1, 8):
+        zs[d - 1].wait_recv()
+        total = total + zr_ref[d]
+    zf_ref[e] = total
+    za = [
+        push(zf_ref.at[e], zf_ref.at[e], za_s.at[d], za_r.at[d], (p, (e + d) % 8))
+        for d in range(1, 8)
+    ]
+    ring_send(5)
+    for c in za:
+        c.wait_recv()
+    for t in range(TILE7):
+        for k in range(4):
+            rel_ref[core, k, off[k], t] = zf_ref[t, k]
+
+    def gather_send(k, s):
+        half = 8 >> s
+        span = rel_ref.at[core, k, pl.ds(offs[k][s], half)]
+        moves[k] = push(span, span, ag_s.at[k, s], ag_r.at[k, s], partner[order[k][s]])
+
+    def gather_step(s):
+        for k in range(4):
+            moves[k].wait_recv()
+            if s > 0:
+                gather_send(k, s - 1)
+            else:
+                span = rel_ref.at[core, k]
+                moves[k] = push(span, span, last_s.at[k], last_r.at[k], sibling)
+
+    for k in range(4):
+        gather_send(k, 3)
+    gather_step(3)
+    ring_send(6)
+    gather_step(2)
+
+    for half in range(2):
+        parts = []
+        for i, (row, down) in enumerate(streams):
+            if down == half:
+                ring[i].wait_recv()
+                parts.append(ring_ref[i, 6] + g_ref[e, pl.ds(row, RINGS), :])
+        full = jnp.concatenate(
+            [parts[0][:HALF], parts[1][:HALF], jnp.zeros((56, CHUNK), jnp.float32)], axis=0
+        ).T
+        for n in range(32):
+            out_ref[n, half] = full[n * 8:(n + 1) * 8, :]
+    swap = [
+        push(out_ref.at[(p + d) % 32], ent_ref.at[p], a2a_s.at[d], a2a_r.at[d], ((p + d) % 32, e))
+        for d in range(1, 32)
+    ]
+    ent_ref[p] = out_ref[p]
+    gather_step(1)
+    gather_step(0)
+    for c in swap:
+        c.wait_recv()
+    for k in range(4):
+        moves[k].wait_recv()
+    for c in sent:
+        c.wait_send()
+
+
+def exchange(g, r):
+    vmem = pl.BlockSpec(memory_space=pltpu.VMEM)
+    f32 = jnp.float32
+    dma = pltpu.SemaphoreType.DMA
+    return pl.pallas_call(
+        exchange_kernel,
+        out_shape=(
+            jax.ShapeDtypeStruct((32, 2, 8, CHUNK), f32),
+            jax.ShapeDtypeStruct((2, 4, 16, TILE7, 8, 128), f32),
+        ),
+        in_specs=[vmem] * 2,
+        out_specs=(vmem, vmem),
+        scratch_shapes=[
+            pltpu.VMEM((4, 7, RINGS, CHUNK), f32),
+            pltpu.VMEM((4, 16, TILE7, 8, 128), f32),
+            pltpu.VMEM((4, 16, TILE7, 8, 128), f32),
+            pltpu.VMEM((4, 15, TILE7, 8, 128), f32),
+            pltpu.VMEM((8, 4, 8, 128), f32),
+            pltpu.VMEM((8, 4, 8, 128), f32),
+            pltpu.VMEM((8, 4, 8, 128), f32),
+            pltpu.VMEM((32, 2, 8, CHUNK), f32),
+            dma((4, 7)), dma((4, 7)), dma((4,)), dma((4,)), dma((4, 4)), dma((4, 4)),
+            dma((8,)), dma((8,)), dma((8,)), dma((8,)),
+            dma((4, 4)), dma((4, 4)), dma((4,)), dma((4,)), dma((32,)), dma((32,)),
+        ],
+        compiler_params=pltpu.CompilerParams(
+            collective_id=0, has_side_effects=True, vmem_limit_bytes=48 * 1024 * 1024
+        ),
+        name="exchange",
+    )(g, r)
+
+
+def finish_kernel(plan_ref, ent_ref, rel_ref, out_ref, rel_out_ref):
+    def put(i, c):
+        out_ref[plan_ref[i]] = ent_ref[i][:, :DIM]
+        return c
+
+    lax.fori_loop(0, 64, put, 0, unroll=8)
+
+    def turn(n):
+        v = rel_ref[pl.ds(n * 26, 26)].reshape(FEAT, 128)
+        v = jnp.concatenate([v[:HALF], v[HPAD:HPAD + HALF], jnp.zeros((56, 128), jnp.float32)], axis=0)
+        return v.T[:, :DIM]
+
+    def rows(n, c):
+        rel_out_ref[pl.ds(pl.multiple_of(n * 128, 128), 128), :] = turn(n)
+        return c
+
+    lax.fori_loop(0, 32, rows, 0, unroll=4)
+    rel_out_ref[4096:NREL, :] = turn(32)[: NREL - 4096]
+
+
+def finish(plan, ent, rel):
+    vmem = pl.BlockSpec(memory_space=pltpu.VMEM)
+    return pl.pallas_call(
+        finish_kernel,
+        out_shape=(
+            jax.ShapeDtypeStruct((64, 8, DIM), jnp.float32),
+            jax.ShapeDtypeStruct((NREL, DIM), jnp.float32),
+        ),
+        in_specs=[pl.BlockSpec(memory_space=pltpu.SMEM), vmem, vmem],
+        out_specs=(vmem, vmem),
+        compiler_params=pltpu.CompilerParams(vmem_limit_bytes=32 * 1024 * 1024),
+        name="finish",
+    )(plan, ent, rel)
 
 
 def local(entities, relations, edge_src, edge_rel, edge_dst, negatives, pair_live, pair_plan):
-    pair_count = lax.axis_size("pair")
     edge_index = lax.axis_index("edge")
     outgoing = halves(entities[jnp.transpose(pair_plan)])
     arrived = lax.all_to_all(outgoing, "pair", split_axis=1, concat_axis=1, tiled=True)
@@ -250,13 +505,8 @@
         blocks[0], blocks[1], relations, edge_src[0], edge_rel[0], edge_dst[0], negatives[0],
         pair_live[0], edge_index * SLOTS,
     )
-    summed = lax.psum_scatter(ent, "edge", scatter_dimension=1, tiled=True)
-    rows = jnp.transpose(summed.reshape(2, FEAT, CHUNK), (0, 2, 1)).reshape(2, pair_count, 8, FEAT)
-    returned = lax.all_to_all(rows, "pair", split_axis=1, concat_axis=1, tiled=True)
-    where = jnp.argsort(jnp.transpose(pair_plan).reshape(-1))
-    ent_grad = unhalve(returned.reshape(2 * pair_count, 8, FEAT)[where])
-    rel_grad = lax.psum(unhalve(rel.T)[:NREL], ("pair", "edge"))
-    return ent_grad, rel_grad
+    returned, rel_tiles = exchange(ent, rel.reshape(2, 4, 16, TILE7, 8, 128))
+    return finish(pair_plan.reshape(-1), returned.reshape(64, 8, CHUNK), rel_tiles.reshape(896, 8, 128))
 
 
 def solution(mesh):

time: 498 us -> 265 us (0.53)
  waiting for transfers between devices: 327 us -> 23.4 us
  Pallas kernels: 93.5 us -> 174 us
  starting transfers between devices: 16.4 us -> 8.63 us
  other arithmetic: 12.4 us -> 7.29 us
    psum x1 -> x0, waiting for transfers between devices: 246 us -> none  [local(): rel_grad = lax.psum(unhalve(rel.T)[:NREL], ('pair', 'edge'))]
    pallas_call x1 -> x3, Pallas kernels: 93.5 us -> 174 us  [the longest x1 93.7 us: edge_call(): pl.pallas_call(edge_kernel, out_shape=(jax.ShapeDtypeStruct((8, 2 * FEAT,...]
    reduce_scatter x1 -> x0, waiting for transfers between devices: 47.3 us -> none  [local(): summed = lax.psum_scatter(ent, 'edge', scatter_dimension=1, tiled=True)]
    all_to_all x1 -> x0, waiting for transfers between devices: 9.44 us -> none  [local(): lax.all_to_all(rows, 'pair', split_axis=1, concat_axis=1, tiled=True)]
    all_to_all x1 -> x0, starting transfers between devices: 7.68 us -> none  [local(): lax.all_to_all(rows, 'pair', split_axis=1, concat_axis=1, tiled=True)]
    pallas_call x0 -> x1, local copies, waits for them, and re-layouts: none -> 5.36 us  [finish(): pl.pallas_call(finish_kernel, out_shape=(jax.ShapeDtypeStruct((64, 8, DIM...]
  transfers between devices with their start and end apart: 5 -> 2, of which waited for: 5 -> 2; matrix products, arithmetic and copies ran while one was open for 7% -> 9% of each run, Pallas kernels for 0% -> 0%
where the time goes in v2:
time: 265 us; the launch traced here: 264 us
  Pallas kernels  174 us (66%)
  local copies, waits for them, and re-layouts  35.1 us (13%)
  waiting for transfers between devices  23.4 us (9%)
  between operations  14.8 us (6%)
  starting transfers between devices  8.63 us (3%)
  other arithmetic  7.29 us (3%)
    pallas_call x1, Pallas kernels, edge_call(): pl.pallas_call(edge_kernel, out_shape=(jax.ShapeDtypeStruct((8, 2 * FEAT,...  93.7 us
    pallas_call x1, Pallas kernels, exchange(): pl.pallas_call(exchange_kernel, out_shape=(jax.ShapeDtypeStruct((32, 2, 8...  77.8 us
    all_gather x1, waiting for transfers between devices, local(): blocks = lax.all_gather(owned, 'edge', axis=2, tiled=True)  16.5 us
    reshape x2, local copies, waits for them, and re-layouts, rel_table(): relations.reshape(NREL, 2, HALF)  11.5 us
    all_to_all x1, starting transfers between devices, local(): lax.all_to_all(outgoing, 'pair', split_axis=1, concat_axis=1, tiled=True)  8.59 us
    all_to_all x1, waiting for transfers between devices, local(): lax.all_to_all(outgoing, 'pair', split_axis=1, concat_axis=1, tiled=True)  6.84 us
    pad x1, local copies, waits for them, and re-layouts, rel_table(): jnp.pad(relations.reshape(NREL, 2, HALF), ((0, 0), (0, 0), (0, 128 - HALF)))  6.57 us
    unnamed x17, local copies, waits for them, and re-layouts  6.16 us
  transfers between devices with their start and end apart: 2, of which 2 were waited for; matrix products, arithmetic and copies ran while one was open for 9% of the time, Pallas kernels for 0%

profile of v2, /device:TPU:1, one launch (start us, length us, event | category | flops | bytes accessed | tf_op | source)
XLA Modules:
  0.0 263.9 jit_solution(376472412478074989)
XLA Ops:
  7.2 0.7 compare_select_fusion
  8.0 0.1 copy-done
  8.1 0.6 gather_fusion
  8.7 0.1 slice.20
  8.8 0.7 slice_select_fusion
  9.5 0.1 fusion.7
  9.7 0.7 copy.49
  10.4 8.6 %all-to-all-start = ((bf16[2,32,8,208]{3,2,0,1:T(8,128)(2,1)}), bf16[2,32,8,208]{3,2,0,1:T(8,128)(2,1)S(1)}, u32[]{:S(2)}, u32[]{:S(2)}) async-start(bf16[2,32,8,208]{3,2,0,1:T(8,128)(2,1)} %copy.49), calls=%async_computation | async-start | bytes 524288 | tf_op jit(solution)/shard_map/all_to_all | solution.py:501
  19.0 1.4 fusion.12
  21.1 6.8 %all-to-all-done = bf16[2,32,8,208]{3,2,0,1:T(8,128)(2,1)S(1)} async-done(((bf16[2,32,8,208]{3,2,0,1:T(8,128)(2,1)}), bf16[2,32,8,208]{3,2,0,1:T(8,128)(2,1)S(1)}, u32[]{:S(2)}, u32[]{:S(2)}) %all-to-all-start) | async-done | bytes 213024 | tf_op jit(solution)/shard_map/all_to_all | solution.py:501
  28.0 0.8 copy.51
  29.0 0.2 convert_reduce_fusion
  29.3 0.1 reduce.1
  29.7 4.0 %reshape.293 = f32[4131,2,100]{0,2,1:T(8,128)} reshape(f32[4131,200]{0,1:T(8,128)} %param.9) | data formatting | bytes 6609600 | tf_op jit(solution)/shard_map/reshape | solution.py:223
  33.7 7.5 %copy.52 = f32[4131,2,100]{2,1,0:T(2,128)} copy(f32[4131,2,100]{0,2,1:T(8,128)} %reshape.293) | data formatting | bytes 6609600 | tf_op jit(solution)/shard_map/reshape | solution.py:223
  41.2 6.6 %pad.13.table_ref = f32[4131,2,128]{2,1,0:T(2,128)} pad(f32[4131,2,100]{2,1,0:T(2,128)} %copy.52, f32[]{:T(128)} %constant.53.clone.1), padding=0_0x0_0x0_28 | pad | bytes 7534948 | tf_op jit(solution)/shard_map/jit(_pad)/pad | solution.py:223
  47.9 0.7 maximum_convert_fusion.tile_ref
  48.6 0.6 pad_add_fusion.meta_ref
  49.2 0.2 fusion.2
  49.4 0.6 convert_bitcast_fusion.pos_ref
  50.0 0.7 add_bitcast_fusion.neg_ref
  50.7 0.6 and_add_fusion
  51.3 0.6 and_add_fusion.1
  52.0 16.5 %all-gather.2.cloned.1.call-done = bf16[2,208,2048]{2,1,0:T(8,128)(2,1)} async-done(((bf16[2,208,256]{2,1,0:T(8,128)(2,1)}), bf16[2,208,2048]{2,1,0:T(8,128)(2,1)}) %all-gather.2.cloned.1.call-update) | async-done | bytes 1703952 | tf_op jit(solution)/shard_map/all_gather | solution.py:503
  68.5 2.8 %slice_bitcast_fusion = (bf16[208,2048]{1,0:T(8,128)(2,1)}, bf16[208,2048]{1,0:T(8,128)(2,1)}) fusion(bf16[2,208,2048]{2,1,0:T(8,128)(2,1)} %all-gather.2.cloned.1.call-done), kind=kLoop, calls=%fused_computation.5 | loop fusion | bytes 3407872 | tf_op jit(solution)/shard_map/squeeze | solution.py:505
  71.3 93.7 %edges.1 = (f32[8,416,256]{2,1,0:T(8,128)}, f32[896,8,128]{2,1,0:T(8,128)}) custom-call(s32[2]{0:T(128)} %pad_add_fusion.meta_ref, s32[4096]{0:T(1024)} %bitcast.46, s32[4096]{0:T(1024)} %convert_bitcast_fusion.pos_ref, s32[34]{0:T(128)} %maximum_convert_fusion.tile_ref, s32[8,1,512]{2,1,0:T(1,128)} %bitcast.49, s32[8,1,512]{2,1,0:T(1,128)} %bitcast.48, ...), custom_call_target="tpu_custom_call" | custom-call | tf_op jit(solution)/shard_map/edges/pallas_call | solution.py:173
  165.0 2.0 copy-done.3
  166.9 77.8 %exchange.1 = (f32[32,2,8,256]{3,2,1,0:T(8,128)S(1)}, f32[2,4,16,7,8,128]{5,4,3,2,1,0:T(8,128)}) custom-call(f32[8,416,256]{2,1,0:T(8,128)S(1)} %copy-done.3, f32[2,4,16,7,8,128]{5,4,3,2,1,0:T(8,128)} %bitcast.41), custom_call_target="tpu_custom_call" | custom-call | tf_op jit(solution)/shard_map/exchange/pallas_call | solution.py:435
  244.8 2.0 copy-done.2
  246.8 2.9 %finish.1 = (f32[64,8,200]{2,1,0:T(8,128)}, f32[4131,200]{1,0:T(8,128)S(1)}) custom-call(s32[64]{0:T(128)S(1)} %reshape.289.plan_ref, f32[64,8,256]{2,1,0:T(8,128)S(1)} %bitcast.40, f32[896,8,128]{2,1,0:T(8,128)S(1)} %bitcast.39), custom_call_target="tpu_custom_call" | custom-call | tf_op jit(solution)/shard_map/finish/pallas_call | solution.py:485
  249.7 1.9 copy-done.1
  251.7 5.4 %copy.53 = f32[4131,200]{0,1:T(8,128)} copy(f32[4131,200]{1,0:T(8,128)} %copy-done.1) | data formatting | bytes 6609600 | tf_op jit(solution)/shard_map/finish/pallas_call | solution.py:485
  (27 shorter events, 0.8 us)
Async XLA Ops:
  7.2 1.0 copy-start
  7.2 21.7 %copy-start.7 = (s32[32,2]{0,1:T(2,128)S(1)}, s32[32,2]{0,1:T(2,128)}, u32[]{:S(2)}) copy-start(s32[32,2]{0,1:T(2,128)} %param.15) | copy-start | bytes 772
  10.4 17.6 %all-to-all-start = ((bf16[2,32,8,208]{3,2,0,1:T(8,128)(2,1)}), bf16[2,32,8,208]{3,2,0,1:T(8,128)(2,1)S(1)}, u32[]{:S(2)}, u32[]{:S(2)}) async-start(bf16[2,32,8,208]{3,2,0,1:T(8,128)(2,1)} %copy.49), calls=%async_computation | async-start | bytes 524288 | tf_op jit(solution)/shard_map/all_to_all | solution.py:501
  19.0 49.5 %all-gather.2.cloned.1.call-start = ((), (), s32[]{:S(2)}) async-start(), calls=%async_computation.1 | async-start | bytes 1916928 | tf_op jit(solution)/shard_map/all_gather | solution.py:503
  41.2 8.8 %copy-start.4 = (s32[1,8,1024]{2,1,0:T(8,128)S(1)}, s32[1,8,1024]{2,1,0:T(8,128)}, u32[]{:S(2)}) copy-start(s32[1,8,1024]{2,1,0:T(8,128)} %param.13) | copy-start | bytes 98308
  41.2 9.5 %copy-start.5 = (s32[1,4096]{1,0:T(1,128)S(1)}, s32[1,4096]{1,0:T(1,128)}, u32[]{:S(2)}) copy-start(s32[1,4096]{1,0:T(1,128)} %param.12) | copy-start | bytes 49156
  41.2 10.1 %copy-start.6 = (s32[1,4096]{1,0:T(1,128)S(1)}, s32[1,4096]{1,0:T(1,128)}, u32[]{:S(2)}) copy-start(s32[1,4096]{1,0:T(1,128)} %param.10) | copy-start | bytes 49156
  165.0 2.0 copy-start.3
  244.8 2.0 copy-start.2
  249.7 2.0 copy-start.1
Sparse Core Ops, SparseCore 0:
  29.0 39.4 all-gather.1

commit v3 on v2

--- a/solution.py
+++ b/solution.py
@@ -33,29 +33,29 @@
     return jnp.concatenate([hi, lo], axis=0)
 
 
+def place(ids):
+    owner = ids // 64
+    left = ids - owner * 64
+    edge = left // 8
+    return edge * 256 + owner * 8 + (left - edge * 8)
+
+
 def edge_kernel(
-    meta_ref, relid_ref, pos_ref, tile_ref,
-    src_ref, dst_ref, neg_ref, relf_ref, s_ref, t_ref, table_ref,
+    live_ref, pos_ref, tile_ref,
+    src_ref, dst_ref, neg_ref, relid_ref, tab_ref, tn_ref, xy_ref,
     ent_ref, rel_ref,
-    tn_ref, sc_ref, w_ref, ohs_ref, ohd_ref, ct_ref, rows_ref, perm_ref, sort_ref,
+    sc_ref, w_ref, ohs_ref, ohd_ref, ct_ref, perm_ref, sort_ref,
 ):
-    live_blocks = meta_ref[0]
-    live_here = meta_ref[1]
+    live_here = live_ref[0] - lax.axis_index("edge") * SLOTS
     ent_ref[...] = jnp.zeros_like(ent_ref)
-    for h in range(ROWS // CHUNK):
-        part = t_ref[:, h * CHUNK:(h + 1) * CHUNK].astype(jnp.float32)
-        part = jnp.concatenate([part, jnp.zeros((256 - FEAT, CHUNK), jnp.float32)], axis=0)
-        tn_ref[h * CHUNK:(h + 1) * CHUNK, :] = part.T.astype(jnp.bfloat16)
+    s_ref = tab_ref.at[0]
+    t_ref = tab_ref.at[1]
 
     def block(b, carry):
-        def fetch_row(j, c):
-            rows_ref[j] = table_ref[relid_ref[b * SPAN + j]]
-            return c
-
-        lax.fori_loop(0, SPAN, fetch_row, 0, unroll=16)
-        src_row = src_ref[b]
-        dst_row = dst_ref[b]
-        neg_row = neg_ref[b]
+        at = pl.ds(pl.multiple_of(b * SPAN, SPAN), SPAN)
+        src_row = place(src_ref[:, at])
+        dst_row = place(dst_ref[:, at])
+        neg_row = place(neg_ref[0, pl.ds(b, 1), :])
         for h in range(ROWS // CHUNK):
             ids = lax.broadcasted_iota(jnp.int32, (CHUNK, SPAN), 0) + h * CHUNK
             at = pl.ds(h * CHUNK, CHUNK)
@@ -74,8 +74,8 @@
 
         source = mm(s_ref[...], ohs_ref[...])
         target = mm(t_ref[...], ohd_ref[...])
-        x = rows_ref[:, 0, :].T[:HPAD]
-        y = rows_ref[:, 1, :].T[:HPAD]
+        x = xy_ref[b, :HPAD]
+        y = xy_ref[b, HPAD:]
         a, c = source[:HPAD], source[HPAD:]
         query_b = jnp.concatenate(
             [a * x - c * y, a * y + c * x, jnp.zeros((256 - FEAT, SPAN), jnp.float32)], axis=0
@@ -112,7 +112,7 @@
         pos_q = split2(coef * query)
         g, k = grad_q[:HPAD], grad_q[HPAD:]
         grad_s = split2(jnp.concatenate([g * x + k * y, k * x - g * y], axis=0))
-        relrow = relf_ref[b]
+        relrow = relid_ref[:, pl.ds(pl.multiple_of(b * SPAN, SPAN), SPAN)].astype(jnp.float32)
         first = lax.broadcasted_iota(jnp.int32, (24, SPAN), 0) == 0
         perm_ref[:, 0, :] = jnp.concatenate(
             [g * a + k * c, jnp.where(first, relrow, 0.0)], axis=0
@@ -121,11 +121,12 @@
             [k * a - g * c, jnp.zeros((24, SPAN), jnp.float32)], axis=0
         ).T
 
-        def place_row(j, cc):
-            sort_ref[pos_ref[b * SPAN + j]] = perm_ref[j]
-            return cc
-
-        lax.fori_loop(0, SPAN, place_row, 0, unroll=16)
+        for n in range(SPAN // 128):
+            def place_row(j, cc, n=n):
+                sort_ref[pos_ref[b * (SPAN // 128) + n, j]] = perm_ref[n * 128 + j]
+                return cc
+
+            lax.fori_loop(0, 128, place_row, 0, unroll=16)
         for h in range(8):
             at = slice(h * CHUNK, (h + 1) * CHUNK)
             oh = ohs_ref[at, :]
@@ -137,11 +138,11 @@
             ent_ref[h, FEAT:, :] += neg * count + (pos[:FEAT] + pos[FEAT:])
         return carry
 
-    lax.fori_loop(0, live_blocks, block, 0)
+    lax.fori_loop(0, live_blocks_of(live_here), block, 0)
 
     def tile(t, carry):
-        begin = tile_ref[t]
-        size = tile_ref[RTILES + t]
+        begin = tile_ref[t, 0]
+        size = tile_ref[t, 1]
 
         def piece(n, acc):
             base = begin + n * RTILE
@@ -167,7 +168,7 @@
     rel_ref[884:] = jnp.zeros((12, 8, 128), jnp.float32)
 
 
-def edge_call(meta, relid, pos, tiles, src, dst, neg, relf, s_t, t_t, table):
+def edge_call(live, pos, tiles, src, dst, neg, relid, tab, tn, xy):
     smem = pl.BlockSpec(memory_space=pltpu.SMEM)
     vmem = pl.BlockSpec(memory_space=pltpu.VMEM)
     return pl.pallas_call(
@@ -176,66 +177,201 @@
             jax.ShapeDtypeStruct((8, 2 * FEAT, CHUNK), jnp.float32),
             jax.ShapeDtypeStruct((896, 8, 128), jnp.float32),
         ),
-        in_specs=[smem] * 4 + [vmem] * 7,
+        in_specs=[smem] * 3 + [vmem] * 7,
         out_specs=(vmem, vmem),
         scratch_shapes=[
-            pltpu.VMEM((ROWS, 256), jnp.bfloat16),
             pltpu.VMEM((ROWS, SPAN), jnp.float32),
             pltpu.VMEM((ROWS, SPAN), jnp.bfloat16),
             pltpu.VMEM((ROWS, SPAN), jnp.bfloat16),
             pltpu.VMEM((ROWS, SPAN), jnp.bfloat16),
             pltpu.VMEM((2 * FEAT, ROWS), jnp.bfloat16),
             pltpu.VMEM((SPAN, 2, 128), jnp.float32),
-            pltpu.VMEM((SPAN, 2, 128), jnp.float32),
             pltpu.VMEM((SLOTS + RTILE, 2, 128), jnp.float32),
         ],
         compiler_params=pltpu.CompilerParams(vmem_limit_bytes=56 * 1024 * 1024),
         name="edges",
-    )(meta, relid, pos, tiles, src, dst, neg, relf, s_t, t_t, table)
-
-
-def place(ids):
-    return ((ids >> 3) & 7) * 256 + (ids >> 6) * 8 + (ids & 7)
-
-
-def bucket(relid, live_blocks):
-    which = relid >> 8
-    valid = (jnp.arange(SLOTS, dtype=jnp.int32) < live_blocks * SPAN)[:, None]
-    one = ((which[:, None] == jnp.arange(RTILES, dtype=jnp.int32)[None]) & valid).astype(jnp.bfloat16)
-    grid = one.reshape(SLOTS // 128, 128, RTILES)
-    tri = (jnp.arange(128)[:, None] > jnp.arange(128)[None]).astype(jnp.bfloat16)
-    inner = jnp.einsum("ij,cjt->cit", tri, grid, preferred_element_type=jnp.float32)
-    sums = jnp.sum(grid.astype(jnp.float32), axis=1)
-    outer = jnp.cumsum(sums, axis=0) - sums
-    size = jnp.sum(sums, axis=0)
-    begin = jnp.cumsum(size) - size
-    where = inner + (outer + begin[None])[:, None, :]
-    pos = jnp.sum(where * grid.astype(jnp.float32), axis=2).reshape(SLOTS).astype(jnp.int32)
-    return pos, jnp.concatenate([begin, size]).astype(jnp.int32)
-
-
-def halves(v):
-    pad = [(0, 0)] * (v.ndim - 1) + [(0, HPAD - HALF)]
-    return jnp.concatenate([jnp.pad(v[..., :HALF], pad), jnp.pad(v[..., HALF:], pad)], axis=-1)
-
-
-def rel_table(relations):
-    return jnp.pad(relations.reshape(NREL, 2, HALF), ((0, 0), (0, 0), (0, 128 - HALF)))
-
-
-def edge_work(s_t, t_t, relations, edge_src, edge_rel, edge_dst, negatives, live_count, first_slot):
-    live_here = live_count - first_slot
-    live_blocks = jnp.clip((live_here + SPAN - 1) // SPAN, 0, SPANS_DEV)
-    meta = jnp.stack([live_blocks, live_here])
-    pos, tiles = bucket(edge_rel, live_blocks)
-    return edge_call(
-        meta, edge_rel, pos, tiles,
-        place(edge_src).reshape(SPANS_DEV, 1, SPAN),
-        place(edge_dst).reshape(SPANS_DEV, 1, SPAN),
-        place(negatives).reshape(SPANS_DEV, 1, 1024),
-        edge_rel.astype(jnp.float32).reshape(SPANS_DEV, 1, SPAN),
-        s_t, t_t, rel_table(relations),
+    )(live, pos, tiles, src, dst, neg, relid, tab, tn, xy)
+
+
+def fetch_kernel(
+    plan_ref, relid_ref, live_ref, relrow_ref, ent_ref, rel_hbm,
+    tab_ref, tn_ref, xy_ref, pos_ref, tile_ref,
+    relt_ref, table_ref, rows_ref, stage_ref, got_ref, ag_ref,
+    rel_sem, a2a_s, a2a_r, ag_s, ag_r,
+):
+    p = lax.axis_index("pair")
+    e = lax.axis_index("edge")
+    load = pltpu.make_async_copy(rel_hbm, relt_ref, rel_sem)
+    load.start()
+    barrier = pltpu.get_barrier_semaphore()
+    for d in range(1, 32):
+        pl.semaphore_signal(barrier, inc=1, device_id=((p + d) % 32, e), device_id_type=MESH)
+    for d in (1, 7):
+        pl.semaphore_signal(barrier, inc=1, device_id=(p, (e + d) % 8), device_id_type=MESH)
+
+    gap = jnp.zeros((16, 256 - DIM), jnp.float32)
+
+    def stage(n, c):
+        both = jnp.concatenate(
+            [ent_ref[plan_ref[0, n]].astype(jnp.float32), ent_ref[plan_ref[1, n]].astype(jnp.float32)], axis=0
+        )
+        stage_ref[n] = jnp.concatenate([both, gap], axis=1).astype(jnp.bfloat16)
+        return c
+
+    lax.fori_loop(0, 32, stage, 0, unroll=4)
+    pl.semaphore_wait(barrier, 33)
+    sent = []
+
+    def push(src, dst, ss, rs, device):
+        copy = pltpu.make_async_remote_copy(
+            src_ref=src, dst_ref=dst, send_sem=ss, recv_sem=rs, device_id=device, device_id_type=MESH
+        )
+        copy.start()
+        sent.append(copy)
+        return copy
+
+    swap = [
+        push(stage_ref.at[(p + d) % 32], got_ref.at[p], a2a_s.at[d], a2a_r.at[d], ((p + d) % 32, e))
+        for d in range(1, 32)
+    ]
+    got_ref[p] = stage_ref[p]
+
+    valid = live_blocks_of(live_ref[0] - e * SLOTS) * SPAN
+    ones = []
+    total = jnp.zeros((32, 1), jnp.float32)
+    sub = lax.broadcasted_iota(jnp.int32, (32, 128), 0)
+    lane = lax.broadcasted_iota(jnp.int32, (32, 128), 1)
+    for c in range(32):
+        which = relrow_ref[:, c * 128:(c + 1) * 128] // RTILE
+        one = jnp.where((sub == which) & (lane + c * 128 < valid), 1.0, 0.0)
+        size = jnp.sum(one, axis=1, keepdims=True)
+        ones.append((one, size))
+        total = total + size
+    below = jnp.where(
+        lax.broadcasted_iota(jnp.int32, (32, 32), 1) < lax.broadcasted_iota(jnp.int32, (32, 32), 0), 1.0, 0.0
     )
+    begin = lax.dot_general(
+        below, jnp.broadcast_to(total, (32, 128)), NN,
+        precision=lax.Precision.HIGHEST, preferred_element_type=jnp.float32,
+    )
+    tile_ref[...] = jnp.where(lane == 0, begin, total).astype(jnp.int32)
+    ahead = jnp.where(
+        lax.broadcasted_iota(jnp.int32, (128, 128), 0) < lax.broadcasted_iota(jnp.int32, (128, 128), 1), 1.0, 0.0
+    ).astype(jnp.bfloat16)
+    for c in range(32):
+        one, size = ones[c]
+        place = one * (mm(one.astype(jnp.bfloat16), ahead) + begin)
+        pos_ref[c:c + 1, :] = jnp.sum(place, axis=0, keepdims=True).astype(jnp.int32)
+        begin = begin + size
+
+    load.wait()
+
+    def turn(n, v):
+        v = jnp.concatenate([v, jnp.zeros((28, 128), jnp.float32)], axis=0)
+        w = jnp.concatenate([v[HALF:DIM], jnp.zeros((28, 128), jnp.float32)], axis=0)
+        table_ref[pl.ds(n * 128, 128), 0, :] = v[:128].T
+        table_ref[pl.ds(n * 128, 128), 1, :] = w.T
+
+    def build(n, c):
+        turn(n, relt_ref[:, pl.ds(pl.multiple_of(n * 128, 128), 128)])
+        return c
+
+    lax.fori_loop(0, 32, build, 0, unroll=4)
+    tail = jnp.concatenate([relt_ref[:, 4096:NREL], jnp.zeros((DIM, 4224 - NREL), jnp.float32)], axis=1)
+    turn(32, tail)
+
+    for c in swap:
+        c.wait_recv()
+    for s in range(2):
+        rows = got_ref[...].astype(jnp.float32)[:, s * 8:(s + 1) * 8, :].reshape(CHUNK, 256)
+        cols = rows.T
+        zero = jnp.zeros((HPAD - HALF, CHUNK), jnp.float32)
+        ag_ref[e, s] = jnp.concatenate([cols[:HALF], zero, cols[HALF:DIM], zero], axis=0).astype(jnp.bfloat16)
+
+    hops = {}
+
+    def forward(h, way, s):
+        o = (e + 8 - (h - 1)) % 8 if way == 0 else (e + (h - 1)) % 8
+        to = (p, (e + 1) % 8) if way == 0 else (p, (e + 7) % 8)
+        hops[way, s] = push(
+            ag_ref.at[o, s], ag_ref.at[o, s], ag_s.at[way, s, h - 1], ag_r.at[way, s, h - 1], to
+        )
+
+    def settle(o):
+        at = pl.ds(pl.multiple_of(o * CHUNK, CHUNK), CHUNK)
+        tab_ref[0, :, at] = ag_ref[o, 0]
+        tab_ref[1, :, at] = ag_ref[o, 1]
+        part = ag_ref[o, 1].astype(jnp.float32)
+        part = jnp.concatenate([part, jnp.zeros((256 - FEAT, CHUNK), jnp.float32)], axis=0)
+        tn_ref[at, :] = part.T.astype(jnp.bfloat16)
+
+    def relations_of(b):
+        def fetch_row(j, c):
+            rows_ref[j] = table_ref[relid_ref[0, b * SPAN + j]]
+            return c
+
+        lax.fori_loop(0, SPAN, fetch_row, 0, unroll=16)
+        xy_ref[b, :HPAD] = jnp.where(keep, rows_ref[:, 0, :].T[:HPAD], 0.0)
+        xy_ref[b, HPAD:] = rows_ref[:, 1, :].T[:HPAD]
+
+    keep = lax.broadcasted_iota(jnp.int32, (HPAD, SPAN), 0) < HALF
+    all_streams = [(0, 0), (1, 1), (0, 1), (1, 0)]
+    for way, s in all_streams:
+        forward(1, way, s)
+    settle(e)
+    relations_of(0)
+    relations_of(1)
+    for h in range(1, 4):
+        for way, s in all_streams:
+            hops[way, s].wait_recv()
+            if h < 3 or way == s:
+                forward(h + 1, way, s)
+        settle((e + 8 - h) % 8)
+        settle((e + h) % 8)
+        relations_of(2 * h)
+        relations_of(2 * h + 1)
+    hops[0, 0].wait_recv()
+    hops[1, 1].wait_recv()
+    settle((e + 4) % 8)
+    for c in sent:
+        c.wait_send()
+
+
+def live_blocks_of(live_here):
+    return jnp.clip((live_here + SPAN - 1) // SPAN, 0, SPANS_DEV)
+
+
+def fetch(plan, relid, live, entities, relations_t):
+    smem = pl.BlockSpec(memory_space=pltpu.SMEM)
+    vmem = pl.BlockSpec(memory_space=pltpu.VMEM)
+    f32 = jnp.float32
+    bf16 = jnp.bfloat16
+    dma = pltpu.SemaphoreType.DMA
+    return pl.pallas_call(
+        fetch_kernel,
+        out_shape=(
+            jax.ShapeDtypeStruct((2, FEAT, ROWS), bf16),
+            jax.ShapeDtypeStruct((ROWS, 256), bf16),
+            jax.ShapeDtypeStruct((SPANS_DEV, FEAT, SPAN), f32),
+            jax.ShapeDtypeStruct((32, 128), jnp.int32),
+            jax.ShapeDtypeStruct((32, 128), jnp.int32),
+        ),
+        in_specs=[smem, smem, smem, vmem, vmem, pl.BlockSpec(memory_space=pl.ANY)],
+        out_specs=(vmem,) * 5,
+        scratch_shapes=[
+            pltpu.VMEM((DIM, NREL), f32),
+            pltpu.VMEM((4224, 2, 128), f32),
+            pltpu.VMEM((SPAN, 2, 128), f32),
+            pltpu.VMEM((32, 16, 256), bf16),
+            pltpu.VMEM((32, 16, 256), bf16),
+            pltpu.VMEM((8, 2, FEAT, CHUNK), bf16),
+            dma, dma((32,)), dma((32,)), dma((2, 2, 4)), dma((2, 2, 4)),
+        ],
+        compiler_params=pltpu.CompilerParams(
+            collective_id=1, has_side_effects=True, vmem_limit_bytes=48 * 1024 * 1024
+        ),
+        name="fetch",
+    )(plan, relid, live, relid, entities, relations_t)
 
 
 RINGS = 104
@@ -462,22 +598,22 @@
 
 def finish_kernel(plan_ref, ent_ref, rel_ref, out_ref, rel_out_ref):
     def put(i, c):
-        out_ref[plan_ref[i]] = ent_ref[i][:, :DIM]
+        out_ref[plan_ref[0, i]] = ent_ref[2 * i][:, :DIM]
+        out_ref[plan_ref[1, i]] = ent_ref[2 * i + 1][:, :DIM]
         return c
 
-    lax.fori_loop(0, 64, put, 0, unroll=8)
-
-    def turn(n):
+    lax.fori_loop(0, 32, put, 0, unroll=4)
+
+    def tile(n):
         v = rel_ref[pl.ds(n * 26, 26)].reshape(FEAT, 128)
-        v = jnp.concatenate([v[:HALF], v[HPAD:HPAD + HALF], jnp.zeros((56, 128), jnp.float32)], axis=0)
-        return v.T[:, :DIM]
+        return jnp.concatenate([v[:HALF], v[HPAD:HPAD + HALF]], axis=0)
 
     def rows(n, c):
-        rel_out_ref[pl.ds(pl.multiple_of(n * 128, 128), 128), :] = turn(n)
+        rel_out_ref[:, pl.ds(pl.multiple_of(n * 128, 128), 128)] = tile(n)
         return c
 
     lax.fori_loop(0, 32, rows, 0, unroll=4)
-    rel_out_ref[4096:NREL, :] = turn(32)[: NREL - 4096]
+    rel_out_ref[:, 4096:NREL] = tile(32)[:, :NREL - 4096]
 
 
 def finish(plan, ent, rel):
@@ -486,7 +622,7 @@
         finish_kernel,
         out_shape=(
             jax.ShapeDtypeStruct((64, 8, DIM), jnp.float32),
-            jax.ShapeDtypeStruct((NREL, DIM), jnp.float32),
+            jax.ShapeDtypeStruct((DIM, NREL), jnp.float32),
         ),
         in_specs=[pl.BlockSpec(memory_space=pltpu.SMEM), vmem, vmem],
         out_specs=(vmem, vmem),
@@ -496,17 +632,12 @@
 
 
 def local(entities, relations, edge_src, edge_rel, edge_dst, negatives, pair_live, pair_plan):
-    edge_index = lax.axis_index("edge")
-    outgoing = halves(entities[jnp.transpose(pair_plan)])
-    arrived = lax.all_to_all(outgoing, "pair", split_axis=1, concat_axis=1, tiled=True)
-    owned = jnp.transpose(arrived.reshape(2, CHUNK, FEAT), (0, 2, 1))
-    blocks = lax.all_gather(owned, "edge", axis=2, tiled=True)
-    ent, rel = edge_work(
-        blocks[0], blocks[1], relations, edge_src[0], edge_rel[0], edge_dst[0], negatives[0],
-        pair_live[0], edge_index * SLOTS,
-    )
+    plan = pair_plan.T
+    tab, tn, xy, pos, tiles = fetch(plan, edge_rel, pair_live, entities, relations.T)
+    ent, rel = edge_call(pair_live, pos, tiles, edge_src, edge_dst, negatives, edge_rel, tab, tn, xy)
     returned, rel_tiles = exchange(ent, rel.reshape(2, 4, 16, TILE7, 8, 128))
-    return finish(pair_plan.reshape(-1), returned.reshape(64, 8, CHUNK), rel_tiles.reshape(896, 8, 128))
+    ent_grad, rel_grad = finish(plan, returned.reshape(64, 8, CHUNK), rel_tiles.reshape(896, 8, 128))
+    return ent_grad, rel_grad.T
 
 
 def solution(mesh):

time: 265 us -> 216 us (0.82)
  Pallas kernels: 174 us -> 205 us
  local copies, waits for them, and re-layouts: 35.1 us -> 9.71 us
  waiting for transfers between devices: 23.4 us -> 0 us
  between operations: 14.8 us -> 1.33 us
  starting transfers between devices: 8.63 us -> 0 us
  other arithmetic: 7.29 us -> 0 us
    pallas_call x0 -> x1, Pallas kernels: none -> 37.7 us  [fetch(): pl.pallas_call(fetch_kernel, out_shape=(jax.ShapeDtypeStruct((2, FEAT, RO...]
    all_gather x1 -> x0, waiting for transfers between devices: 16.5 us -> none  [local(): blocks = lax.all_gather(owned, 'edge', axis=2, tiled=True)]
    reshape x4 -> x0, local copies, waits for them, and re-layouts: 12.4 us -> none  [the longest x2 11.5 us: rel_table(): relations.reshape(NREL, 2, HALF)]
    all_to_all x1 -> x0, starting transfers between devices: 8.59 us -> none  [local(): lax.all_to_all(outgoing, 'pair', split_axis=1, concat_axis=1, tiled=True)]
    all_to_all x1 -> x0, waiting for transfers between devices: 6.84 us -> none  [local(): lax.all_to_all(outgoing, 'pair', split_axis=1, concat_axis=1, tiled=True)]
    pad x1 -> x0, local copies, waits for them, and re-layouts: 6.57 us -> none  [rel_table(): jnp.pad(relations.reshape(NREL, 2, HALF), ((0, 0), (0, 0), (0, 128 - HALF)))]
    pallas_call x1 -> x0, local copies, waits for them, and re-layouts: 5.36 us -> none  [finish(): pl.pallas_call(finish_kernel, out_shape=(jax.ShapeDtypeStruct((64, 8, DIM...]
    pallas_call x1, Pallas kernels: 93.7 us -> 89.8 us  [edge_call(): pl.pallas_call(edge_kernel, out_shape=(jax.ShapeDtypeStruct((8, 2 * FEAT,...]
  transfers between devices with their start and end apart: 2 -> 0, of which waited for: 2 -> 0; matrix products, arithmetic and copies ran while one was open for 9% -> 0% of each run, Pallas kernels for 0% -> 0%
where the time goes in v3:
time: 216 us
  Pallas kernels  205 us (95%)
  local copies, waits for them, and re-layouts  9.71 us (4%)
    pallas_call x1, Pallas kernels, edge_call(): pl.pallas_call(edge_kernel, out_shape=(jax.ShapeDtypeStruct((8, 2 * FEAT,...  89.8 us
    pallas_call x1, Pallas kernels, exchange(): pl.pallas_call(exchange_kernel, out_shape=(jax.ShapeDtypeStruct((32, 2, 8...  74.4 us
    pallas_call x1, Pallas kernels, fetch(): pl.pallas_call(fetch_kernel, out_shape=(jax.ShapeDtypeStruct((2, FEAT, RO...  37.7 us
    unnamed x20, local copies, waits for them, and re-layouts  9.71 us

profile of v3, /device:TPU:1, one launch (start us, length us, event | category | flops | bytes accessed | tf_op | source)
XLA Modules:
  0.0 215.8 jit_solution(18003951639270302675)
XLA Ops:
  1.3 0.0 copy-start.4
  1.3 0.9 copy-done.4
  2.2 0.0 copy-start.5
  2.2 0.7 copy-done.5
  2.9 0.0 copy-start.8
  2.9 0.7 copy-done.8
  3.6 37.7 %fetch.1 = (bf16[2,208,2048]{2,1,0:T(8,128)(2,1)S(1)}, bf16[2048,256]{1,0:T(8,128)(2,1)S(1)}, f32[8,208,512]{2,1,0:T(8,128)}, s32[32,128]{1,0:T(8,128)S(1)}, s32[32,128]{1,0:T(8,128)S(1)}) custom-call(s32[2,32]{1,0:T(2,128)S(1)} %bitcast.8, s32[1,4096]{1,0:T(1,128)S(1)} %copy-done.5, s32[1]{0:T(128)S(6)} %copy.10.live_ref, s32[1,4096]{1,0:T(1,128)S(1)} %copy-done.5, ...), custom_call_target="tpu_custom_call" | custom-call | tf_op jit(solution)/shard_map/fetch/pallas_call | solution.py:350
  41.3 0.0 copy-start.2
  41.3 1.2 copy-done.2
  42.5 0.0 copy-start.3
  42.5 1.0 copy-done.3
  43.5 0.0 copy-start.6
  43.5 0.6 copy-done.6
  44.1 0.0 copy-start.7
  44.1 0.6 copy-done.7
  44.7 89.8 %edges.1 = (f32[8,416,256]{2,1,0:T(8,128)}, f32[896,8,128]{2,1,0:T(8,128)}) custom-call(s32[1]{0:T(128)S(6)} %copy.10.live_ref, s32[32,128]{1,0:T(8,128)} %copy-done.6, s32[32,128]{1,0:T(8,128)} %copy-done.7, s32[1,4096]{1,0:T(1,128)} %src_ref.1, s32[1,4096]{1,0:T(1,128)} %dst_ref.1, s32[1,8,1024]{2,1,0:T(8,128)} %neg_ref.1, s32[1,4096]{1,0:T(1,128)} %relid_ref.3, ...), custom_call_target="tpu_custom_call" | custom-call | tf_op jit(solution)/shard_map/edges/pallas_call | solution.py:174
  134.5 0.0 copy-start.1
  134.5 2.0 copy-done.1
  136.5 0.0 copy-start.9
  136.5 74.4 %exchange.1 = (f32[32,2,8,256]{3,2,1,0:T(8,128)S(1)}, f32[2,4,16,7,8,128]{5,4,3,2,1,0:T(8,128)}) custom-call(f32[8,416,256]{2,1,0:T(8,128)S(1)} %copy-done.1, f32[2,4,16,7,8,128]{5,4,3,2,1,0:T(8,128)} %bitcast.10), custom_call_target="tpu_custom_call" | custom-call | tf_op jit(solution)/shard_map/exchange/pallas_call | solution.py:571
  210.9 0.0 copy-done.9
  210.9 0.0 copy-start
  210.9 2.0 copy-done
  213.0 2.9 %finish.1 = (f32[64,8,200]{2,1,0:T(8,128)}, f32[200,4131]{1,0:T(8,128)}) custom-call(s32[2,32]{1,0:T(2,128)S(1)} %bitcast.9, f32[64,8,256]{2,1,0:T(8,128)S(1)} %bitcast.7, f32[896,8,128]{2,1,0:T(8,128)S(1)} %bitcast.6), custom_call_target="tpu_custom_call" | custom-call | tf_op jit(solution)/shard_map/finish/pallas_call | solution.py:621
Async XLA Ops:
  1.3 1.0 copy-start.4
  2.2 0.7 copy-start.5
  2.9 0.7 copy-start.8
  41.3 1.2 copy-start.2
  42.5 1.0 copy-start.3
  43.5 0.6 copy-start.6
  44.1 0.6 copy-start.7
  134.5 2.0 copy-start.1
  136.5 74.4 %copy-start.9 = (s32[32,2]{0,1:T(2,128)S(1)}, s32[32,2]{0,1:T(2,128)}, u32[]{:S(2)}) copy-start(s32[32,2]{0,1:T(2,128)} %param.15) | copy-start | bytes 772
  210.9 2.0 copy-start

commit v4 on v3

--- a/solution.py
+++ b/solution.py
@@ -18,6 +18,7 @@
 SLOTS = SPAN * SPANS_DEV
 ROWS = 2048
 CHUNK = 256
+WIDE = 384
 NN = (((1,), (0,)), ((), ()))
 NT = (((1,), (1,)), ((), ()))
 MESH = pl.DeviceIdType.MESH
@@ -121,15 +122,11 @@
             [k * a - g * c, jnp.zeros((24, SPAN), jnp.float32)], axis=0
         ).T
 
-        for n in range(SPAN // 128):
-            def place_row(j, cc, n=n):
-                sort_ref[pos_ref[b * (SPAN // 128) + n, j]] = perm_ref[n * 128 + j]
-                return cc
-
-            lax.fori_loop(0, 128, place_row, 0, unroll=16)
         for h in range(8):
             at = slice(h * CHUNK, (h + 1) * CHUNK)
             oh = ohs_ref[at, :]
+            for j in range(h * 64, h * 64 + 64):
+                sort_ref[pos_ref[b * SPAN + j]] = perm_ref[j]
             back = mm(grad_s, oh, NT)
             ent_ref[h, :FEAT, :] += back[:FEAT] + back[FEAT:]
             neg = mm(query_b[:FEAT], w_ref[at, :], NT)
@@ -140,29 +137,33 @@
 
     lax.fori_loop(0, live_blocks_of(live_here), block, 0)
 
+    def piece(t, n):
+        left = tile_ref[t, 1] - n * WIDE
+        base = tile_ref[t, 0] + n * WIDE
+        ok = lax.broadcasted_iota(jnp.int32, (WIDE, 128), 0) < left
+        re = jnp.where(ok, sort_ref[pl.ds(base, WIDE), 0, :], 0.0).T
+        im = jnp.where(ok, sort_ref[pl.ds(base, WIDE), 1, :], 0.0).T
+        names = re[HPAD:HPAD + 1, :].astype(jnp.int32)
+        oh = jnp.where(
+            lax.broadcasted_iota(jnp.int32, (RTILE, WIDE), 0) + t * RTILE == names, 1.0, 0.0
+        ).astype(jnp.bfloat16)
+        part = mm(split2(jnp.concatenate([re[:HPAD], im[:HPAD]], axis=0)), oh, NT)
+        part = part[:FEAT] + part[FEAT:]
+        return part[:, :128].reshape(26, 8, 128), part[:, 128:].reshape(26, 8, 128)
+
+    for t in range(RTILES):
+        one, two = piece(t, 0)
+        rel_ref[52 * t:52 * t + 26] = one
+        rel_ref[52 * t + 26:52 * t + 52] = two
+
     def tile(t, carry):
-        begin = tile_ref[t, 0]
-        size = tile_ref[t, 1]
-
-        def piece(n, acc):
-            base = begin + n * RTILE
-            left = size - n * RTILE
-            ok = lax.broadcasted_iota(jnp.int32, (RTILE, 128), 0) < left
-            re = jnp.where(ok, sort_ref[pl.ds(base, RTILE), 0, :], 0.0).T
-            im = jnp.where(ok, sort_ref[pl.ds(base, RTILE), 1, :], 0.0).T
-            names = re[HPAD:HPAD + 1, :].astype(jnp.int32)
-            oh = jnp.where(
-                lax.broadcasted_iota(jnp.int32, (RTILE, RTILE), 0) + t * RTILE == names, 1.0, 0.0
-            ).astype(jnp.bfloat16)
-            part = mm(split2(jnp.concatenate([re[:HPAD], im[:HPAD]], axis=0)), oh, NT)
-            return acc + part[:FEAT] + part[FEAT:]
-
-        acc = lax.fori_loop(
-            0, (size + RTILE - 1) // RTILE, piece, jnp.zeros((FEAT, RTILE), jnp.float32)
-        )
-        rel_ref[pl.ds(52 * t, 26)] = acc[:, :128].reshape(26, 8, 128)
-        rel_ref[pl.ds(52 * t + 26, 26)] = acc[:, 128:].reshape(26, 8, 128)
-        return carry
+        def more(n, c):
+            one, two = piece(t, n)
+            rel_ref[pl.ds(52 * t, 26)] += one
+            rel_ref[pl.ds(52 * t + 26, 26)] += two
+            return c
+
+        return lax.fori_loop(1, (tile_ref[t, 1] + WIDE - 1) // WIDE, more, carry)
 
     lax.fori_loop(0, RTILES, tile, 0)
     rel_ref[884:] = jnp.zeros((12, 8, 128), jnp.float32)
@@ -186,7 +187,7 @@
             pltpu.VMEM((ROWS, SPAN), jnp.bfloat16),
             pltpu.VMEM((2 * FEAT, ROWS), jnp.bfloat16),
             pltpu.VMEM((SPAN, 2, 128), jnp.float32),
-            pltpu.VMEM((SLOTS + RTILE, 2, 128), jnp.float32),
+            pltpu.VMEM((SLOTS + WIDE, 2, 128), jnp.float32),
         ],
         compiler_params=pltpu.CompilerParams(vmem_limit_bytes=56 * 1024 * 1024),
         name="edges",
@@ -368,7 +369,7 @@
             dma, dma((32,)), dma((32,)), dma((2, 2, 4)), dma((2, 2, 4)),
         ],
         compiler_params=pltpu.CompilerParams(
-            collective_id=1, has_side_effects=True, vmem_limit_bytes=48 * 1024 * 1024
+            collective_id=1, has_side_effects=True, vmem_limit_bytes=56 * 1024 * 1024
         ),
         name="fetch",
     )(plan, relid, live, relid, entities, relations_t)
@@ -379,7 +380,8 @@
 
 
 def exchange_kernel(
-    g_ref, r_ref, ent_ref, rel_ref,
+    g_hbm, r_hbm, ent_ref, rel_ref,
+    g_ref, r_ref, load_s,
     ring_ref, core_ref, acc_ref, hyp_ref, zb_ref, zr_ref, zf_ref, out_ref,
     ring_s, ring_r, core_s, core_r, hyp_s, hyp_r, zs_s, zs_r, za_s, za_r,
     ag_s, ag_r, last_s, last_r, a2a_s, a2a_r,
@@ -413,6 +415,10 @@
         ("y2", "x1", "y1", "x2"),
     ]
     sibling = (p + 1 - 2 * core, e)
+    load_r = pltpu.make_async_copy(r_hbm.at[core], r_ref, load_s.at[0])
+    load_r.start()
+    load_g = pltpu.make_async_copy(g_hbm, g_ref, load_s.at[1])
+    load_g.start()
 
     barrier = pltpu.get_barrier_semaphore()
     for d in range(1, 32):
@@ -441,7 +447,7 @@
         for i, (row, down) in enumerate(streams):
             c = chunk(down, s)
             if s == 0:
-                src = g_ref.at[c, pl.ds(row, RINGS)]
+                src = g_hbm.at[c, pl.ds(row, RINGS)]
             else:
                 ring[i].wait_recv()
                 ring_ref[i, s - 1] += g_ref[c, pl.ds(row, RINGS), :]
@@ -450,93 +456,118 @@
             ring[i] = push(src, ring_ref.at[i, s], ring_s.at[i, s], ring_r.at[i, s], to)
 
     moves = {}
-    off = [0, 0, 0, 0]
-    offs = [[], [], [], []]
+    off = {(k, q): 0 for k in range(4) for q in range(2)}
+    offs = {(k, q): [] for k in range(4) for q in range(2)}
     base = [0, 8, 12, 14]
 
-    def hyp_send(k, s):
+    chains = [(k, q) for q in range(2) for k in range(4)]
+    cut = [pl.ds(0, 4), pl.ds(4, 3)]
+
+    def hyp_send(k, q, s):
         half = 8 >> s
         b = bit[order[k][s]]
-        moves[k] = push(
-            acc_ref.at[k, pl.ds(off[k] + (1 - b) * half, half)],
-            hyp_ref.at[k, pl.ds(base[s], half)],
-            hyp_s.at[k, s], hyp_r.at[k, s], partner[order[k][s]],
+        moves[k, q] = push(
+            acc_ref.at[k, pl.ds(off[k, q] + (1 - b) * half, half), cut[q]],
+            hyp_ref.at[k, pl.ds(base[s], half), cut[q]],
+            hyp_s.at[k, q, s], hyp_r.at[k, q, s], partner[order[k][s]],
         )
-        off[k] = off[k] + b * half
-        offs[k].append(off[k])
-
-    def hyp_take(k, s):
+        off[k, q] = off[k, q] + b * half
+        offs[k, q].append(off[k, q])
+
+    def hyp_take(k, q, s):
         half = 8 >> s
-        moves[k].wait_recv()
-        acc_ref[k, pl.ds(off[k], half)] += hyp_ref[k, pl.ds(base[s], half)]
-
-    cores = [
-        push(r_ref.at[1 - core, k], core_ref.at[k], core_s.at[k], core_r.at[k], sibling)
-        for k in range(4)
-    ]
+        moves[k, q].wait_recv()
+        at = (k, pl.ds(off[k, q], half), cut[q])
+        acc_ref[at] += hyp_ref[k, pl.ds(base[s], half), cut[q]]
+
+    cores = {
+        (k, q): push(
+            r_hbm.at[1 - core, k, :, cut[q]], core_ref.at[k, :, cut[q]],
+            core_s.at[k, q], core_r.at[k, q], sibling,
+        )
+        for k, q in chains
+    }
     ring_send(0)
-    for k in range(4):
-        cores[k].wait_recv()
-        acc_ref[k] = r_ref[core, k] + core_ref[k]
-        hyp_send(k, 0)
+    load_r.wait()
+    for k, q in chains:
+        cores[k, q].wait_recv()
+        acc_ref[k, :, cut[q]] = r_ref[k, :, cut[q]] + core_ref[k, :, cut[q]]
+        hyp_send(k, q, 0)
+    load_g.wait()
     ring_send(1)
 
     def hyp_step(s):
-        for k in range(4):
-            hyp_take(k, s)
+        for k, q in chains:
+            hyp_take(k, q, s)
             if s < 3:
-                hyp_send(k, s + 1)
+                hyp_send(k, q, s + 1)
 
     hyp_step(0)
     ring_send(2)
     hyp_step(1)
     hyp_step(2)
     ring_send(3)
-    hyp_step(3)
-    for t in range(TILE7):
+    tiles = [[(t, k) for t in range(4) for k in range(4)], [(t, k) for t in range(4, 7) for k in range(4)]]
+    zmoves = [None, None]
+    zb_ref[1, 6:] = jnp.zeros((2, 2, 8, 128), jnp.float32)
+
+    def z_send(q):
         for k in range(4):
-            zb_ref[t, k] = acc_ref[k, off[k], t]
-    zb_ref[TILE7] = jnp.zeros((4, 8, 128), jnp.float32)
-    zs = [
-        push(zb_ref.at[(e + d) % 8], zr_ref.at[d], zs_s.at[d], zs_r.at[d], (p, (e + d) % 8))
-        for d in range(1, 8)
-    ]
+            hyp_take(k, q, 3)
+        for i, (t, k) in enumerate(tiles[q]):
+            zb_ref[q, i // 2, i % 2] = acc_ref[k, off[k, q], t]
+        zmoves[q] = [
+            push(
+                zb_ref.at[q, (e + d) % 8], zr_ref.at[q, d], zs_s.at[q, d], zs_r.at[q, d], (p, (e + d) % 8)
+            )
+            for d in range(1, 8)
+        ]
+
+    def z_sum(q):
+        total = zb_ref[q, e]
+        for d in range(1, 8):
+            zmoves[q][d - 1].wait_recv()
+            total = total + zr_ref[q, d]
+        zf_ref[q, e] = total
+        zmoves[q] = [
+            push(zf_ref.at[q, e], zf_ref.at[q, e], za_s.at[q, d], za_r.at[q, d], (p, (e + d) % 8))
+            for d in range(1, 8)
+        ]
+
+    def z_spread(q):
+        for c in zmoves[q]:
+            c.wait_recv()
+        for i, (t, k) in enumerate(tiles[q]):
+            rel_ref[core, k, off[k, q], t] = zf_ref[q, i // 2, i % 2]
+        for k in range(4):
+            gather_send(k, q, 3)
+
+    def gather_send(k, q, s):
+        half = 8 >> s
+        span = rel_ref.at[core, k, pl.ds(offs[k, q][s], half), cut[q]]
+        moves[k, q] = push(span, span, ag_s.at[k, q, s], ag_r.at[k, q, s], partner[order[k][s]])
+
+    def gather_step(s):
+        for k, q in chains:
+            moves[k, q].wait_recv()
+            if s > 0:
+                gather_send(k, q, s - 1)
+            else:
+                span = rel_ref.at[core, k, :, cut[q]]
+                moves[k, q] = push(span, span, last_s.at[k, q], last_r.at[k, q], sibling)
+
+    z_send(0)
+    z_send(1)
     ring_send(4)
-    total = zb_ref[e]
-    for d in range(1, 8):
-        zs[d - 1].wait_recv()
-        total = total + zr_ref[d]
-    zf_ref[e] = total
-    za = [
-        push(zf_ref.at[e], zf_ref.at[e], za_s.at[d], za_r.at[d], (p, (e + d) % 8))
-        for d in range(1, 8)
-    ]
+    z_sum(0)
+    z_sum(1)
+    z_spread(0)
+    z_spread(1)
     ring_send(5)
-    for c in za:
-        c.wait_recv()
-    for t in range(TILE7):
-        for k in range(4):
-            rel_ref[core, k, off[k], t] = zf_ref[t, k]
-
-    def gather_send(k, s):
-        half = 8 >> s
-        span = rel_ref.at[core, k, pl.ds(offs[k][s], half)]
-        moves[k] = push(span, span, ag_s.at[k, s], ag_r.at[k, s], partner[order[k][s]])
-
-    def gather_step(s):
-        for k in range(4):
-            moves[k].wait_recv()
-            if s > 0:
-                gather_send(k, s - 1)
-            else:
-                span = rel_ref.at[core, k]
-                moves[k] = push(span, span, last_s.at[k], last_r.at[k], sibling)
-
-    for k in range(4):
-        gather_send(k, 3)
     gather_step(3)
+    gather_step(2)
     ring_send(6)
-    gather_step(2)
+    gather_step(1)
 
     for half in range(2):
         parts = []
@@ -554,12 +585,11 @@
         for d in range(1, 32)
     ]
     ent_ref[p] = out_ref[p]
-    gather_step(1)
     gather_step(0)
     for c in swap:
         c.wait_recv()
-    for k in range(4):
-        moves[k].wait_recv()
+    for k, q in chains:
+        moves[k, q].wait_recv()
     for c in sent:
         c.wait_send()
 
@@ -574,23 +604,26 @@
             jax.ShapeDtypeStruct((32, 2, 8, CHUNK), f32),
             jax.ShapeDtypeStruct((2, 4, 16, TILE7, 8, 128), f32),
         ),
-        in_specs=[vmem] * 2,
+        in_specs=[pl.BlockSpec(memory_space=pl.ANY)] * 2,
         out_specs=(vmem, vmem),
         scratch_shapes=[
+            pltpu.VMEM((8, 2 * FEAT, CHUNK), f32),
+            pltpu.VMEM((4, 16, TILE7, 8, 128), f32),
+            dma((2,)),
             pltpu.VMEM((4, 7, RINGS, CHUNK), f32),
             pltpu.VMEM((4, 16, TILE7, 8, 128), f32),
             pltpu.VMEM((4, 16, TILE7, 8, 128), f32),
             pltpu.VMEM((4, 15, TILE7, 8, 128), f32),
-            pltpu.VMEM((8, 4, 8, 128), f32),
-            pltpu.VMEM((8, 4, 8, 128), f32),
-            pltpu.VMEM((8, 4, 8, 128), f32),
+            pltpu.VMEM((2, 8, 2, 8, 128), f32),
+            pltpu.VMEM((2, 8, 2, 8, 128), f32),
+            pltpu.VMEM((2, 8, 2, 8, 128), f32),
             pltpu.VMEM((32, 2, 8, CHUNK), f32),
-            dma((4, 7)), dma((4, 7)), dma((4,)), dma((4,)), dma((4, 4)), dma((4, 4)),
-            dma((8,)), dma((8,)), dma((8,)), dma((8,)),
-            dma((4, 4)), dma((4, 4)), dma((4,)), dma((4,)), dma((32,)), dma((32,)),
+            dma((4, 7)), dma((4, 7)), dma((4, 2)), dma((4, 2)), dma((4, 2, 4)), dma((4, 2, 4)),
+            dma((2, 8)), dma((2, 8)), dma((2, 8)), dma((2, 8)),
+            dma((4, 2, 4)), dma((4, 2, 4)), dma((4, 2)), dma((4, 2)), dma((32,)), dma((32,)),
         ],
         compiler_params=pltpu.CompilerParams(
-            collective_id=0, has_side_effects=True, vmem_limit_bytes=48 * 1024 * 1024
+            collective_id=0, has_side_effects=True, vmem_limit_bytes=56 * 1024 * 1024
         ),
         name="exchange",
     )(g, r)
@@ -634,7 +667,7 @@
 def local(entities, relations, edge_src, edge_rel, edge_dst, negatives, pair_live, pair_plan):
     plan = pair_plan.T
     tab, tn, xy, pos, tiles = fetch(plan, edge_rel, pair_live, entities, relations.T)
-    ent, rel = edge_call(pair_live, pos, tiles, edge_src, edge_dst, negatives, edge_rel, tab, tn, xy)
+    ent, rel = edge_call(pair_live, pos.reshape(SLOTS), tiles, edge_src, edge_dst, negatives, edge_rel, tab, tn, xy)
     returned, rel_tiles = exchange(ent, rel.reshape(2, 4, 16, TILE7, 8, 128))
     ent_grad, rel_grad = finish(plan, returned.reshape(64, 8, CHUNK), rel_tiles.reshape(896, 8, 128))
     return ent_grad, rel_grad.T

time: 216 us -> 181 us (0.84)
  Pallas kernels: 205 us -> 176 us
  local copies, waits for them, and re-layouts: 9.71 us -> 3.08 us
    pallas_call x1, Pallas kernels: 89.8 us -> 68.7 us  [edge_call(): pl.pallas_call(edge_kernel, out_shape=(jax.ShapeDtypeStruct((8, 2 * FEAT,...]
    pallas_call x1, Pallas kernels: 74.4 us -> 65.8 us  [exchange(): pl.pallas_call(exchange_kernel, out_shape=(jax.ShapeDtypeStruct((32, 2, 8...]
    unnamed x20 -> x6, local copies, waits for them, and re-layouts: 9.71 us -> 3.08 us
where the time goes in v4:
time: 181 us
  Pallas kernels  176 us (97%)
  local copies, waits for them, and re-layouts  3.08 us (2%)
    pallas_call x1, Pallas kernels, edge_call(): pl.pallas_call(edge_kernel, out_shape=(jax.ShapeDtypeStruct((8, 2 * FEAT,...  68.7 us
    pallas_call x1, Pallas kernels, exchange(): pl.pallas_call(exchange_kernel, out_shape=(jax.ShapeDtypeStruct((32, 2, 8...  65.8 us
    pallas_call x1, Pallas kernels, fetch(): pl.pallas_call(fetch_kernel, out_shape=(jax.ShapeDtypeStruct((2, FEAT, RO...  38.9 us

profile of v4, /device:TPU:1, one launch (start us, length us, event | category | flops | bytes accessed | tf_op | source)
XLA Modules:
  0.0 180.6 jit_solution(4290109984823277812)
XLA Ops:
  1.3 38.9 %fetch.1 = (bf16[2,208,2048]{2,1,0:T(8,128)(2,1)}, bf16[2048,256]{1,0:T(8,128)(2,1)}, f32[8,208,512]{2,1,0:T(8,128)}, s32[32,128]{1,0:T(8,128)}, s32[32,128]{1,0:T(8,128)}) custom-call(s32[2,32]{1,0:T(2,128)} %bitcast.9, s32[1,4096]{1,0:T(1,128)} %relid_ref.3, s32[1]{0:T(128)S(6)} %copy.10.live_ref, s32[1,4096]{1,0:T(1,128)} %relid_ref.3, ...), custom_call_target="tpu_custom_call" | custom-call | tf_op jit(solution)/shard_map/fetch/pallas_call | solution.py:351
  40.1 68.7 %edges.1 = (f32[8,416,256]{2,1,0:T(8,128)}, f32[896,8,128]{2,1,0:T(8,128)}) custom-call(s32[1]{0:T(128)S(6)} %copy.10.live_ref, s32[4096]{0:T(1024)} %bitcast.13, s32[32,128]{1,0:T(8,128)} %get-tuple-element.14.tile_ref, s32[1,4096]{1,0:T(1,128)} %src_ref.1, s32[1,4096]{1,0:T(1,128)} %dst_ref.1, s32[1,8,1024]{2,1,0:T(8,128)} %neg_ref.1, ...), custom_call_target="tpu_custom_call" | custom-call | tf_op jit(solution)/shard_map/edges/pallas_call | solution.py:175
  108.8 0.0 copy-start.2
  108.8 65.8 %exchange.1 = (f32[32,2,8,256]{3,2,1,0:T(8,128)}, f32[2,4,16,7,8,128]{5,4,3,2,1,0:T(8,128)}) custom-call(f32[8,416,256]{2,1,0:T(8,128)} %get-tuple-element.18.g_hbm, f32[2,4,16,7,8,128]{5,4,3,2,1,0:T(8,128)} %bitcast.11), custom_call_target="tpu_custom_call" | custom-call | tf_op jit(solution)/shard_map/exchange/pallas_call | solution.py:601
  174.6 0.0 copy-done.2
  174.6 0.0 copy-start
  174.6 2.0 %copy-done = f32[2,4,16,7,8,128]{5,4,3,2,1,0:T(8,128)S(1)} copy-done((f32[2,4,16,7,8,128]{5,4,3,2,1,0:T(8,128)S(1)}, f32[2,4,16,7,8,128]{5,4,3,2,1,0:T(8,128)}, u32[]{:S(2)}) %copy-start) | copy-done | bytes 3670040
  176.7 0.0 copy-start.1
  176.7 1.0 copy-done.1
  177.7 2.9 %finish.1 = (f32[64,8,200]{2,1,0:T(8,128)}, f32[200,4131]{1,0:T(8,128)}) custom-call(s32[2,32]{1,0:T(2,128)S(1)} %bitcast.10, f32[64,8,256]{2,1,0:T(8,128)S(1)} %bitcast.8, f32[896,8,128]{2,1,0:T(8,128)S(1)} %bitcast.7), custom_call_target="tpu_custom_call" | custom-call | tf_op jit(solution)/shard_map/finish/pallas_call | solution.py:654
Async XLA Ops:
  108.8 65.8 %copy-start.2 = (s32[32,2]{0,1:T(2,128)S(1)}, s32[32,2]{0,1:T(2,128)}, u32[]{:S(2)}) copy-start(s32[32,2]{0,1:T(2,128)} %param.15) | copy-start | bytes 772
  174.6 2.0 %copy-start = (f32[2,4,16,7,8,128]{5,4,3,2,1,0:T(8,128)S(1)}, f32[2,4,16,7,8,128]{5,4,3,2,1,0:T(8,128)}, u32[]{:S(2)}) copy-start(f32[2,4,16,7,8,128]{5,4,3,2,1,0:T(8,128)} %get-tuple-element.21) | copy-start | bytes 11010052
  176.7 1.0 copy-start.1
